TPU v7x, 32 devices: a whole 2x2x4 slice. The times are simulated.
32 devices in a mesh: blk: 4 (over y, x), tile: 8 (over z, core).
Axes of the slice: x: 2, y: 2, z: 4, core: 2. Of those that a mesh axis runs over, the one named last changes fastest.
Arguments:
- grid_feat: bfloat16 [8192, 512], P(('blk', 'tile')), may hold values from -18 to 18
- queries: bfloat16 [8192, 512], P(('blk', 'tile')), may hold values from -90 to 90
- obs_keys: bfloat16 [256, 512], P(('blk', 'tile')), may hold values from -4 to 4
- obs_values: bfloat16 [256, 512], P(('blk', 'tile')), may hold values from -6 to 6
- block_mask: int32 [64, 2], P(('blk', 'tile')), may hold values from 0 to 1, as said below
- obs_valid: int32 [2], replicated, may hold values from 2 to 128, as said below
- out_weight: bfloat16 [512, 512], replicated, may hold values from -0.25 to 0.25
- conv_weight: bfloat16 [3, 3, 512, 512], replicated, may hold values from -0.09375 to 0.09375
Outputs:
- layer_out: bfloat16 [8192, 512], P(('blk', 'tile'))
Inputs may be any that keep to these rules, and one draw needn't show every extreme that they name: `block_mask`: row t has a 1 in column t mod 2. `obs_valid`: at least one entry equals 128.
All inputs are finite; a program needn't handle non-finite values.
Results may differ from a plain program's by a relative error of at most 0.007.
Values may be sent and summed in bfloat16 or wider, within the bound.
No kernel may reach another device: no remote copies, remote signals or barrier semaphores. Data moves between devices by JAX's collectives and lax.ppermute only.
A program may use at most 64 MiB of HBM per device.

v0:
```python
import functools
import math

import jax
import jax.numpy as jnp
from jax import lax
from jax.experimental import pallas as pl
from jax.experimental.pallas import tpu as pltpu
from jax.sharding import PartitionSpec as P

HEADS = 8
OBS_BLOCK = 128
AXES = ("blk", "tile")
PAIR = 2
CORES = 2
LIMIT_ROWS = 16


def both_cores(same_ref, other_ref, cols):
    return jnp.concatenate(
        [ref[:, :, cols].reshape(-1, cols.stop - cols.start) for ref in (same_ref, other_ref)], axis=0
    )


def attend(lon, width, nblocks, rows, core, row_refs, keys_of, same_ref, other_ref, weight_refs, mixed_ref):
    head = width // HEADS
    pair = PAIR * head
    obs = nblocks * OBS_BLOCK
    scale = head ** (-0.5) * math.log2(math.e)
    half = OBS_BLOCK // CORES
    key_lane = lax.broadcasted_iota(jnp.int32, (1, OBS_BLOCK), 1)
    spread = (key_lane % half) // rows * (CORES * rows) + key_lane % rows
    first = key_lane < half

    def row_bias(ref):
        limit = ref[2 * lon : 2 * lon + LIMIT_ROWS, :].astype(jnp.float32)[:1].astype(jnp.int32)

        parts = []
        for parity in (core, 1 - core):
            place = spread + parity * rows
            for block in range(0, nblocks, CORES):
                ends = [
                    jnp.broadcast_to(limit[:, b : b + 1], (1, OBS_BLOCK)) for b in (block, block + 1)
                ]
                end = jnp.where(first, ends[0], ends[1])
                parts.append(jnp.where(place < end, 0.0, -jnp.inf))
        return jnp.concatenate(parts, axis=1)

    biases = [row_bias(ref) for ref in row_refs]
    lane = lax.broadcasted_iota(jnp.int32, (obs, pair), 1)
    ones = [(lane // head == h).astype(jnp.bfloat16) for h in range(PAIR)]

    empty = jnp.zeros((head, obs), jnp.bfloat16)

    def columns(group):
        return slice(group * pair, (group + 1) * pair)

    def scores_of(group):
        keys = keys_of(columns(group))
        query = jnp.concatenate([ref[:lon, columns(group)] for ref in row_refs], axis=0)
        scores = []
        for h in range(PAIR):
            part = [keys[i * head : (i + 1) * head] if i == h else empty for i in range(PAIR)]
            part = jnp.concatenate(part, axis=0)
            scores.append(jnp.dot(query, part, preferred_element_type=jnp.float32))
        return scores

    def weights_of(scores):
        pieces = []
        for t, bias in enumerate(biases):
            piece = scores[t * lon : (t + 1) * lon] * scale + bias
            top = jnp.max(piece, axis=1, keepdims=True)
            pieces.append(jnp.exp2(piece - top).astype(jnp.bfloat16))
        return jnp.concatenate(pieces, axis=0)

    groups = HEADS // PAIR
    ahead = scores_of(0)
    for group in range(groups):
        scores, ahead = ahead, scores_of(group + 1) if group + 1 < groups else None
        values = both_cores(same_ref, other_ref, columns(groups + group))
        value_parts = jnp.concatenate(
            [jnp.concatenate([values * one, one], axis=1) for one in ones], axis=0
        )
        weights = jnp.concatenate([weights_of(part) for part in scores], axis=1)
        both = jnp.dot(weights, value_parts, preferred_element_type=jnp.float32)
        mixed_ref[:, columns(group)] = (both[:, :pair] / both[:, pair:]).astype(jnp.bfloat16)

    depth = width // len(weight_refs)
    projected = sum(
        jnp.dot(
            mixed_ref[:, i * depth : (i + 1) * depth], ref[...], preferred_element_type=jnp.float32
        )
        for i, ref in enumerate(weight_refs)
    )
    grid = jnp.concatenate([ref[lon : 2 * lon, :] for ref in row_refs], axis=0)
    wide = (grid.astype(jnp.float32) + projected).astype(jnp.bfloat16).astype(jnp.float32)
    normed = wide * lax.rsqrt(jnp.mean(wide * wide, axis=-1, keepdims=True) + 1e-06)
    return wide, normed


def around(parts, lon):
    return pltpu.roll(parts[0], 1, 0) + parts[1] + pltpu.roll(parts[2], lon - 1, 0)


def inner_kernel(
    lon, width, nblocks, rows,
    meta_ref, near_ref, near_sent_ref, far_sent_ref, same_ref, other_ref, upper_ref, lower_ref,
    conv_hbm, done_ref, partial_ref, keys_ref, conv_ref, mixed_ref, field_ref, sems,
):
    core = meta_ref[0]
    copies = [
        pltpu.make_async_copy(conv_hbm.at[source], conv_ref.at[i], sems.at[i])
        for i, source in enumerate((1, 2 - 2 * core, 2 * core))
    ]
    for copy in copies:
        copy.start()

    def keys_of(cols):
        keys = both_cores(same_ref, other_ref, cols).T
        keys_ref[cols, :] = keys
        return keys

    wide, normed = attend(
        lon, width, nblocks, rows, core, (near_ref, near_sent_ref, far_sent_ref), keys_of,
        same_ref, other_ref, (upper_ref, lower_ref), mixed_ref,
    )
    field_ref[...] = normed.astype(jnp.bfloat16)
    for copy in copies:
        copy.wait()
    inputs = jnp.concatenate([field_ref[lon:, :], field_ref[: 2 * lon, :]], axis=1)
    full, open_end = [], []
    for lon_off in range(3):
        taps = conv_ref[:2, lon_off].reshape(2 * width, width)
        term = jnp.dot(inputs, taps, preferred_element_type=jnp.float32)
        full.append(
            term[:lon]
            + jnp.dot(field_ref[2 * lon :, :], conv_ref[2, lon_off], preferred_element_type=jnp.float32)
        )
        open_end.append(term[lon:])
    done_ref[...] = (wide[lon : 2 * lon] + around(full, lon)).astype(jnp.bfloat16)
    partial_ref[...] = wide[2 * lon :] + around(open_end, lon)


def outer_kernel(
    lon, width, nblocks, rows,
    meta_ref, far_ref, same_ref, other_ref, upper_ref, lower_ref, done_ref, partial_ref, keys_ref,
    conv_hbm, out_ref, conv_ref, mixed_ref, sem,
):
    core = meta_ref[0]
    copy = pltpu.make_async_copy(conv_hbm.at[2 * core], conv_ref, sem)
    copy.start()
    _, normed = attend(
        lon, width, nblocks, rows, core, (far_ref,), lambda cols: keys_ref[cols, :],
        same_ref, other_ref, (upper_ref, lower_ref), mixed_ref,
    )
    field = jnp.where(meta_ref[1] > 0, normed, 0.0).astype(jnp.bfloat16)
    copy.wait()
    parts = [
        jnp.dot(field, conv_ref[lon_off], preferred_element_type=jnp.float32) for lon_off in range(3)
    ]
    last = (partial_ref[...] + around(parts, lon)).astype(jnp.bfloat16)
    out_ref[pl.ds(pl.multiple_of((1 - core) * lon, lon), lon), :] = done_ref[...]
    out_ref[pl.ds(pl.multiple_of(core * lon, lon), lon), :] = last


def on_device(
    grid_feat, queries, obs_keys, obs_values, block_mask, obs_valid, out_weight, conv_weight
):
    q_dev, width = queries.shape
    tiles, nblocks = block_mask.shape
    rows = obs_keys.shape[0]
    lon = q_dev // tiles
    obs = nblocks * OBS_BLOCK
    devices = lax.axis_size(AXES)
    pairs = devices // CORES
    me = lax.axis_index(AXES)
    core = me % CORES

    block = jnp.concatenate([obs_keys, obs_values], axis=1)
    groups = [list(range(c, devices, CORES)) for c in range(CORES)]
    same = lax.all_to_all(
        jnp.broadcast_to(block[None], (pairs,) + block.shape), AXES, 0, 0, axis_index_groups=groups
    )
    swap = [(i, i ^ 1) for i in range(devices)]
    across = [(i, i + 1) for i in range(1, devices - 1, CORES)]
    across += [(target, source) for source, target in across]

    query_rows, grid_rows = lax.optimization_barrier(
        (jnp.split(queries, tiles, axis=0), jnp.split(grid_feat, tiles, axis=0))
    )
    limits = jnp.where(block_mask > 0, obs_valid[None], 0).astype(jnp.bfloat16)
    limits = jnp.pad(limits, ((0, 0), (0, width - nblocks)))

    def packed(tile):
        limit = jnp.broadcast_to(limits[tile][None], (LIMIT_ROWS, width))
        return jnp.concatenate([query_rows[tile], grid_rows[tile], limit], axis=0)

    first, last = packed(0), packed(tiles - 1)
    far_sent = jnp.where(core == 0, first, last)
    near_sent = jnp.where(core == 0, last, first)
    far = lax.ppermute(far_sent, AXES, across)
    near = lax.ppermute(near_sent, AXES, swap)
    other = lax.ppermute(same, AXES, swap)
    out_weight, _ = lax.optimization_barrier((out_weight, same))
    upper, lower = lax.optimization_barrier(tuple(jnp.split(out_weight, 2, axis=0)))

    far_exists = (me > 0) & (me < devices - 1)
    meta = jnp.stack([core, far_exists.astype(core.dtype)]).astype(jnp.int32)

    vmem = pl.BlockSpec(memory_space=pltpu.VMEM)
    smem = pl.BlockSpec(memory_space=pltpu.SMEM)
    hbm = pl.BlockSpec(memory_space=pltpu.HBM)
    sizes = (lon, width, nblocks, rows)
    params = pltpu.CompilerParams(vmem_limit_bytes=48 * 2**20)
    tap_flops, row_flops = 2 * lon * width * width, 2 * lon * width * (width + 4 * obs)
    done, partial, keys = pl.pallas_call(
        functools.partial(inner_kernel, *sizes),
        out_shape=[
            jax.ShapeDtypeStruct((lon, width), jnp.bfloat16),
            jax.ShapeDtypeStruct((lon, width), jnp.float32),
            jax.ShapeDtypeStruct((width, obs), jnp.bfloat16),
        ],
        in_specs=[smem] + [vmem] * 7 + [hbm],
        out_specs=[vmem] * 3,
        scratch_shapes=[
            pltpu.VMEM(conv_weight.shape, jnp.bfloat16),
            pltpu.VMEM((3 * lon, width), jnp.bfloat16),
            pltpu.VMEM((3 * lon, width), jnp.bfloat16),
            pltpu.SemaphoreType.DMA((3,)),
        ],
        compiler_params=params,
        cost_estimate=pl.CostEstimate(
            flops=3 * row_flops + 15 * tap_flops, bytes_accessed=2 * conv_weight.size, transcendentals=0
        ),
        name="inner",
    )(meta, near, near_sent, far_sent, same, other, upper, lower, conv_weight)
    return pl.pallas_call(
        functools.partial(outer_kernel, *sizes),
        out_shape=jax.ShapeDtypeStruct((q_dev, width), jnp.bfloat16),
        in_specs=[smem] + [vmem] * 8 + [hbm],
        out_specs=vmem,
        scratch_shapes=[
            pltpu.VMEM(conv_weight.shape[1:], jnp.bfloat16),
            pltpu.VMEM((lon, width), jnp.bfloat16),
            pltpu.SemaphoreType.DMA,
        ],
        compiler_params=params,
        cost_estimate=pl.CostEstimate(
            flops=row_flops + 3 * tap_flops, bytes_accessed=conv_weight.size, transcendentals=0
        ),
        name="outer",
    )(meta, far, same, other, upper, lower, done, partial, keys, conv_weight)


def solution(mesh):
    in_specs = (
        P(AXES, None),
        P(AXES, None),
        P(AXES, None),
        P(AXES, None),
        P(AXES, None),
        P(),
        P(),
        P(),
    )
    return jax.shard_map(
        on_device, mesh=mesh, in_specs=in_specs, out_specs=P(AXES, None), check_vma=False
    )
```

profile of v0, /device:TPU:0, one launch (start us, length us, event | category | flops | bytes accessed | tf_op | source)
XLA Modules:
  0.0 30.6 jit_solution(14117529522867869414)
XLA Ops:
  0.0 0.7 %pad_maximum_fusion.2 = bf16[8,1024]{1,0:T(8,128)(2,1)S(1)} fusion(bf16[8,512]{1,0:T(8,128)(2,1)} %param.11, bf16[8,512]{1,0:T(8,128)(2,1)} %param.10), kind=kLoop, calls=%fused_computation.4 | loop fusion | flops 32768 | bytes 32768 | tf_op jit(solution)/shard_map/concatenate | solution.py:179
  0.7 0.7 %broadcast_in_dim.36 = bf16[16,8,1024]{2,1,0:T(8,128)(2,1)} broadcast(bf16[8,1024]{1,0:T(8,128)(2,1)S(1)} %pad_maximum_fusion.2), dimensions={1,2} | broadcast | bytes 278528 | tf_op jit(solution)/shard_map/broadcast_in_dim | solution.py:182
  1.5 8.3 %all-to-all-start = ((bf16[16,8,1024]{2,1,0:T(8,128)(2,1)}), bf16[16,8,1024]{2,1,0:T(8,128)(2,1)S(1)}, u32[]{:S(2)}, u32[]{:S(2)}) async-start(bf16[16,8,1024]{2,1,0:T(8,128)(2,1)} %broadcast_in_dim.36), calls=%async_computation | async-start | bytes 524288 | tf_op jit(solution)/shard_map/all_to_all | solution.py:181
  9.8 1.1 %fusion.2 = (bf16[128,512]{1,0:T(8,128)(2,1)S(1)}, bf16[128,512]{1,0:T(8,128)(2,1)S(1)}, bf16[128,512]{1,0:T(8,128)(2,1)S(1)}, bf16[128,512]{1,0:T(8,128)(2,1)S(1)}) fusion(bf16[256,512]{1,0:T(8,128)(2,1)} %param.8, bf16[256,512]{1,0:T(8,128)(2,1)} %param.9), kind=kLoop, calls=%fused_computation.11 | loop fusion | bytes 1048576 | tf_op jit(solution)/shard_map/split | solution.py:189
  10.9 0.7 %fusion = bf16[2,2]{1,0:T(2,128)(2,1)S(1)} fusion(s32[2,2]{1,0:T(2,128)} %param.12, s32[2]{0:T(128)} %param.13), kind=kLoop, calls=%fused_computation.8 | loop fusion | flops 12 | bytes 32 | tf_op jit(solution)/shard_map/convert_element_type | solution.py:191
  11.7 0.1 broadcast_select_fusion
  11.8 0.1 collective-permute-start.2
  11.8 0.7 %collective-permute-start = (bf16[272,512]{1,0:T(8,128)(2,1)S(1)}, bf16[272,512]{1,0:T(8,128)(2,1)S(1)}, u32[]{:S(2)}, u32[]{:S(2)}) collective-permute-start(bf16[272,512]{1,0:T(8,128)(2,1)S(1)} %get-tuple-element.28.far_sent_ref), channel_id=1, source_target_pairs={{1,2},{3,4},{5,6},{7,8},{9,10},{11,12},{13,14},{15,16},{17,18},{19... | collective-permute-start | bytes 835592 | tf_op jit(solution)/shard_map/ppermute | solution.py:201
  12.5 7.9 %all-to-all-done.same_ref = bf16[16,8,1024]{2,1,0:T(8,128)(2,1)S(1)} async-done(((bf16[16,8,1024]{2,1,0:T(8,128)(2,1)}), bf16[16,8,1024]{2,1,0:T(8,128)(2,1)S(1)}, u32[]{:S(2)}, u32[]{:S(2)}) %all-to-all-start) | async-done | bytes 262176 | tf_op jit(solution)/shard_map/all_to_all | solution.py:181
  20.5 0.0 collective-permute-start.1
  20.5 0.1 pad_add_fusion.meta_ref
  20.5 1.1 %fusion.1 = (bf16[256,512]{1,0:T(8,128)(2,1)S(1)}, bf16[256,512]{1,0:T(8,128)(2,1)S(1)}) fusion(bf16[512,512]{1,0:T(8,128)(2,1)} %param.14), kind=kLoop, calls=%fused_computation.10 | loop fusion | bytes 1048576 | tf_op jit(solution)/shard_map/split | solution.py:205
  21.6 0.0 collective-permute-done.2.near_ref
  21.6 0.4 %collective-permute-done.1.other_ref = bf16[16,8,1024]{2,1,0:T(8,128)(2,1)S(1)} collective-permute-done((bf16[16,8,1024]{2,1,0:T(8,128)(2,1)S(1)}, bf16[16,8,1024]{2,1,0:T(8,128)(2,1)S(1)}, u32[]{:S(2)}, u32[]{:S(2)}) %collective-permute-start.1) | collective-permute-done | bytes 262176 | tf_op jit(solution)/shard_map/ppermute | solution.py:203
  22.0 4.7 %inner.1 = (bf16[128,512]{1,0:T(8,128)(2,1)S(1)}, f32[128,512]{1,0:T(8,128)S(1)}, bf16[512,256]{1,0:T(8,128)(2,1)S(1)}) custom-call(s32[2]{0:T(128)S(1)} %pad_add_fusion.meta_ref, bf16[272,512]{1,0:T(8,128)(2,1)S(1)} %collective-permute-done.2.near_ref, bf16[272,512]{1,0:T(8,128)(2,1)S(1)} %get-tuple-element.27.near_sent_ref, ...), custom_call_target="tpu_custom_call" | custom-call | flops 1610612736 | bytes 4718592 | tf_op jit(solution)/shard_map/inner/pallas_call | solution.py:216
  26.7 0.0 collective-permute-done.far_ref
  26.7 3.8 %outer.1 = bf16[256,512]{1,0:T(8,128)(2,1)} custom-call(s32[2]{0:T(128)S(1)} %pad_add_fusion.meta_ref, bf16[272,512]{1,0:T(8,128)(2,1)S(1)} %collective-permute-done.far_ref, bf16[16,8,1024]{2,1,0:T(8,128)(2,1)S(1)} %all-to-all-done.same_ref, bf16[16,8,1024]{2,1,0:T(8,128)(2,1)S(1)} %collective-permute-done.1.other_ref, ...), custom_call_target="tpu_custom_call" | custom-call | flops 402653184 | bytes 2359296 | tf_op jit(solution)/shard_map/outer/pallas_call | solution.py:237
  (3 shorter events, 0.0 us)
Async XLA Ops:
  1.5 19.0 %all-to-all-start = ((bf16[16,8,1024]{2,1,0:T(8,128)(2,1)}), bf16[16,8,1024]{2,1,0:T(8,128)(2,1)S(1)}, u32[]{:S(2)}, u32[]{:S(2)}) async-start(bf16[16,8,1024]{2,1,0:T(8,128)(2,1)} %broadcast_in_dim.36), calls=%async_computation | async-start | bytes 524288 | tf_op jit(solution)/shard_map/all_to_all | solution.py:181
  11.8 9.8 %collective-permute-start.2 = (bf16[272,512]{1,0:T(8,128)(2,1)S(1)}, bf16[272,512]{1,0:T(8,128)(2,1)S(1)}, u32[]{:S(2)}, u32[]{:S(2)}) collective-permute-start(bf16[272,512]{1,0:T(8,128)(2,1)S(1)} %get-tuple-element.27.near_sent_ref), channel_id=1, source_target_pairs={{0,1},{1,0},{2,3},{3,2},{4,5},{5,4},{6,7},{7,6},{8,9},{9,8},{10,11... | collective-permute-start | bytes 835592 | tf_op jit(solution)/shard_map/ppermute | solution.py:202
  11.8 14.9 %collective-permute-start = (bf16[272,512]{1,0:T(8,128)(2,1)S(1)}, bf16[272,512]{1,0:T(8,128)(2,1)S(1)}, u32[]{:S(2)}, u32[]{:S(2)}) collective-permute-start(bf16[272,512]{1,0:T(8,128)(2,1)S(1)} %get-tuple-element.28.far_sent_ref), channel_id=1, source_target_pairs={{1,2},{3,4},{5,6},{7,8},{9,10},{11,12},{13,14},{15,16},{17,18},{19... | collective-permute-start | bytes 835592 | tf_op jit(solution)/shard_map/ppermute | solution.py:201
  20.5 1.5 %collective-permute-start.1 = (bf16[16,8,1024]{2,1,0:T(8,128)(2,1)S(1)}, bf16[16,8,1024]{2,1,0:T(8,128)(2,1)S(1)}, u32[]{:S(2)}, u32[]{:S(2)}) collective-permute-start(bf16[16,8,1024]{2,1,0:T(8,128)(2,1)S(1)} %all-to-all-done.same_ref), channel_id=1, source_target_pairs={{0,1},{1,0},{2,3},{3,2},{4,5},{5,4},{6,7},{7,6},{8,9},{9,8},{10,11... | collective-permute-start | bytes 786440 | tf_op jit(solution)/shard_map/ppermute | solution.py:203
where the time goes:
time: 30.9 us; the launch traced here: 30.6 us
  starting transfers between devices  9.06 us (29%)
  Pallas kernels  8.54 us (28%)
  waiting for transfers between devices  8.3 us (27%)
  local copies, waits for them, and re-layouts  2.97 us (10%)
  other arithmetic  1.58 us (5%)
    all_to_all x1, starting transfers between devices, on_device(): lax.all_to_all(jnp.broadcast_to(block[None], (pairs,) + block.shape), AXE...  8.31 us
    all_to_all x1, waiting for transfers between devices, on_device(): lax.all_to_all(jnp.broadcast_to(block[None], (pairs,) + block.shape), AXE...  7.91 us
    pallas_call x1, Pallas kernels, on_device(): pl.pallas_call(functools.partial(inner_kernel, *sizes), out_shape=[jax.Sh...  4.73 us
    pallas_call x1, Pallas kernels, on_device(): pl.pallas_call(functools.partial(outer_kernel, *sizes), out_shape=jax.Sha...  3.82 us
    split x1, local copies, waits for them, and re-layouts, on_device(): jnp.split(grid_feat, tiles, axis=0)  1.13 us
    split x1, local copies, waits for them, and re-layouts, on_device(): jnp.split(out_weight, 2, axis=0)  1.06 us
    broadcast_in_dim x1, local copies, waits for them, and re-layouts, on_device(): jnp.broadcast_to(block[None], (pairs,) + block.shape)  0.73 us
    concatenate x1, other arithmetic, on_device(): block = jnp.concatenate([obs_keys, obs_values], axis=1)  0.72 us
  transfers between devices with their start and end apart: 4, of which 2 were waited for; matrix products, arithmetic and copies ran while one was open for 10% of the time, Pallas kernels for 15%

commit v1 on v0

--- a/solution.py
+++ b/solution.py
@@ -74,15 +74,16 @@
         return jnp.concatenate(pieces, axis=0)
 
     groups = HEADS // PAIR
-    ahead = scores_of(0)
+    scores = [scores_of(group) for group in range(groups)]
+    weights = [
+        jnp.concatenate([weights_of(part) for part in scores[group]], axis=1) for group in range(groups)
+    ]
     for group in range(groups):
-        scores, ahead = ahead, scores_of(group + 1) if group + 1 < groups else None
         values = both_cores(same_ref, other_ref, columns(groups + group))
         value_parts = jnp.concatenate(
             [jnp.concatenate([values * one, one], axis=1) for one in ones], axis=0
         )
-        weights = jnp.concatenate([weights_of(part) for part in scores], axis=1)
-        both = jnp.dot(weights, value_parts, preferred_element_type=jnp.float32)
+        both = jnp.dot(weights[group], value_parts, preferred_element_type=jnp.float32)
         mixed_ref[:, columns(group)] = (both[:, :pair] / both[:, pair:]).astype(jnp.bfloat16)
 
     depth = width // len(weight_refs)
@@ -125,18 +126,22 @@
         same_ref, other_ref, (upper_ref, lower_ref), mixed_ref,
     )
     field_ref[...] = normed.astype(jnp.bfloat16)
-    for copy in copies:
-        copy.wait()
+    copies[0].wait()
+    copies[1].wait()
     inputs = jnp.concatenate([field_ref[lon:, :], field_ref[: 2 * lon, :]], axis=1)
-    full, open_end = [], []
-    for lon_off in range(3):
-        taps = conv_ref[:2, lon_off].reshape(2 * width, width)
-        term = jnp.dot(inputs, taps, preferred_element_type=jnp.float32)
-        full.append(
-            term[:lon]
-            + jnp.dot(field_ref[2 * lon :, :], conv_ref[2, lon_off], preferred_element_type=jnp.float32)
+    terms = [
+        jnp.dot(
+            inputs, conv_ref[:2, lon_off].reshape(2 * width, width), preferred_element_type=jnp.float32
         )
-        open_end.append(term[lon:])
+        for lon_off in range(3)
+    ]
+    copies[2].wait()
+    full = [
+        terms[lon_off][:lon]
+        + jnp.dot(field_ref[2 * lon :, :], conv_ref[2, lon_off], preferred_element_type=jnp.float32)
+        for lon_off in range(3)
+    ]
+    open_end = [term[lon:] for term in terms]
     done_ref[...] = (wide[lon : 2 * lon] + around(full, lon)).astype(jnp.bfloat16)
     partial_ref[...] = wide[2 * lon :] + around(open_end, lon)
 

time: 30.9 us -> 30.6 us (level)
  Pallas kernels: 8.54 us -> 8.19 us
    pallas_call x1, Pallas kernels: 3.82 us -> 3.41 us  [on_device(): pl.pallas_call(functools.partial(outer_kernel, *sizes), out_shape=jax.Sha...]
  transfers between devices with their start and end apart: 4 -> 4, of which waited for: 2 -> 2; matrix products, arithmetic and copies ran while one was open for 10% -> 10% of each run, Pallas kernels for 15% -> 16%
where the time goes in v1:
time: 30.6 us; the launch traced here: 30.2 us
  starting transfers between devices  9.06 us (30%)
  waiting for transfers between devices  8.3 us (27%)
  Pallas kernels  8.19 us (27%)
  local copies, waits for them, and re-layouts  2.97 us (10%)
  other arithmetic  1.58 us (5%)
    all_to_all x1, starting transfers between devices, on_device(): lax.all_to_all(jnp.broadcast_to(block[None], (pairs,) + block.shape), AXE...  8.31 us
    all_to_all x1, waiting for transfers between devices, on_device(): lax.all_to_all(jnp.broadcast_to(block[None], (pairs,) + block.shape), AXE...  7.91 us
    pallas_call x1, Pallas kernels, on_device(): pl.pallas_call(functools.partial(inner_kernel, *sizes), out_shape=[jax.Sh...  4.78 us
    pallas_call x1, Pallas kernels, on_device(): pl.pallas_call(functools.partial(outer_kernel, *sizes), out_shape=jax.Sha...  3.41 us
    split x1, local copies, waits for them, and re-layouts, on_device(): jnp.split(grid_feat, tiles, axis=0)  1.13 us
    split x1, local copies, waits for them, and re-layouts, on_device(): jnp.split(out_weight, 2, axis=0)  1.06 us
    broadcast_in_dim x1, local copies, waits for them, and re-layouts, on_device(): jnp.broadcast_to(block[None], (pairs,) + block.shape)  0.73 us
    concatenate x1, other arithmetic, on_device(): block = jnp.concatenate([obs_keys, obs_values], axis=1)  0.72 us
  transfers between devices with their start and end apart: 4, of which 2 were waited for; matrix products, arithmetic and copies ran while one was open for 10% of the time, Pallas kernels for 16%

profile of v1, /device:TPU:0, one launch (start us, length us, event | category | flops | bytes accessed | tf_op | source)
XLA Modules:
  0.0 30.2 jit_solution(13860780483589611354)
XLA Ops:
  0.0 0.7 %pad_maximum_fusion.2 = bf16[8,1024]{1,0:T(8,128)(2,1)S(1)} fusion(bf16[8,512]{1,0:T(8,128)(2,1)} %param.11, bf16[8,512]{1,0:T(8,128)(2,1)} %param.10), kind=kLoop, calls=%fused_computation.4 | loop fusion | flops 32768 | bytes 32768 | tf_op jit(solution)/shard_map/concatenate | solution.py:184
  0.7 0.7 %broadcast_in_dim.36 = bf16[16,8,1024]{2,1,0:T(8,128)(2,1)} broadcast(bf16[8,1024]{1,0:T(8,128)(2,1)S(1)} %pad_maximum_fusion.2), dimensions={1,2} | broadcast | bytes 278528 | tf_op jit(solution)/shard_map/broadcast_in_dim | solution.py:187
  1.5 8.3 %all-to-all-start = ((bf16[16,8,1024]{2,1,0:T(8,128)(2,1)}), bf16[16,8,1024]{2,1,0:T(8,128)(2,1)S(1)}, u32[]{:S(2)}, u32[]{:S(2)}) async-start(bf16[16,8,1024]{2,1,0:T(8,128)(2,1)} %broadcast_in_dim.36), calls=%async_computation | async-start | bytes 524288 | tf_op jit(solution)/shard_map/all_to_all | solution.py:186
  9.8 1.1 %fusion.2 = (bf16[128,512]{1,0:T(8,128)(2,1)S(1)}, bf16[128,512]{1,0:T(8,128)(2,1)S(1)}, bf16[128,512]{1,0:T(8,128)(2,1)S(1)}, bf16[128,512]{1,0:T(8,128)(2,1)S(1)}) fusion(bf16[256,512]{1,0:T(8,128)(2,1)} %param.8, bf16[256,512]{1,0:T(8,128)(2,1)} %param.9), kind=kLoop, calls=%fused_computation.11 | loop fusion | bytes 1048576 | tf_op jit(solution)/shard_map/split | solution.py:194
  10.9 0.7 %fusion = bf16[2,2]{1,0:T(2,128)(2,1)S(1)} fusion(s32[2,2]{1,0:T(2,128)} %param.12, s32[2]{0:T(128)} %param.13), kind=kLoop, calls=%fused_computation.8 | loop fusion | flops 12 | bytes 32 | tf_op jit(solution)/shard_map/convert_element_type | solution.py:196
  11.7 0.1 broadcast_select_fusion
  11.8 0.1 collective-permute-start.2
  11.8 0.7 %collective-permute-start = (bf16[272,512]{1,0:T(8,128)(2,1)S(1)}, bf16[272,512]{1,0:T(8,128)(2,1)S(1)}, u32[]{:S(2)}, u32[]{:S(2)}) collective-permute-start(bf16[272,512]{1,0:T(8,128)(2,1)S(1)} %get-tuple-element.28.far_sent_ref), channel_id=1, source_target_pairs={{1,2},{3,4},{5,6},{7,8},{9,10},{11,12},{13,14},{15,16},{17,18},{19... | collective-permute-start | bytes 835592 | tf_op jit(solution)/shard_map/ppermute | solution.py:206
  12.5 7.9 %all-to-all-done.same_ref = bf16[16,8,1024]{2,1,0:T(8,128)(2,1)S(1)} async-done(((bf16[16,8,1024]{2,1,0:T(8,128)(2,1)}), bf16[16,8,1024]{2,1,0:T(8,128)(2,1)S(1)}, u32[]{:S(2)}, u32[]{:S(2)}) %all-to-all-start) | async-done | bytes 262176 | tf_op jit(solution)/shard_map/all_to_all | solution.py:186
  20.5 0.0 collective-permute-start.1
  20.5 0.1 pad_add_fusion.meta_ref
  20.5 1.1 %fusion.1 = (bf16[256,512]{1,0:T(8,128)(2,1)S(1)}, bf16[256,512]{1,0:T(8,128)(2,1)S(1)}) fusion(bf16[512,512]{1,0:T(8,128)(2,1)} %param.14), kind=kLoop, calls=%fused_computation.10 | loop fusion | bytes 1048576 | tf_op jit(solution)/shard_map/split | solution.py:210
  21.6 0.0 collective-permute-done.2.near_ref
  21.6 0.4 %collective-permute-done.1.other_ref = bf16[16,8,1024]{2,1,0:T(8,128)(2,1)S(1)} collective-permute-done((bf16[16,8,1024]{2,1,0:T(8,128)(2,1)S(1)}, bf16[16,8,1024]{2,1,0:T(8,128)(2,1)S(1)}, u32[]{:S(2)}, u32[]{:S(2)}) %collective-permute-start.1) | collective-permute-done | bytes 262176 | tf_op jit(solution)/shard_map/ppermute | solution.py:208
  22.0 4.8 %inner.1 = (bf16[128,512]{1,0:T(8,128)(2,1)S(1)}, f32[128,512]{1,0:T(8,128)S(1)}, bf16[512,256]{1,0:T(8,128)(2,1)S(1)}) custom-call(s32[2]{0:T(128)S(1)} %pad_add_fusion.meta_ref, bf16[272,512]{1,0:T(8,128)(2,1)S(1)} %collective-permute-done.2.near_ref, bf16[272,512]{1,0:T(8,128)(2,1)S(1)} %get-tuple-element.27.near_sent_ref, ...), custom_call_target="tpu_custom_call" | custom-call | flops 1610612736 | bytes 4718592 | tf_op jit(solution)/shard_map/inner/pallas_call | solution.py:221
  26.8 0.0 collective-permute-done.far_ref
  26.8 3.4 %outer.1 = bf16[256,512]{1,0:T(8,128)(2,1)} custom-call(s32[2]{0:T(128)S(1)} %pad_add_fusion.meta_ref, bf16[272,512]{1,0:T(8,128)(2,1)S(1)} %collective-permute-done.far_ref, bf16[16,8,1024]{2,1,0:T(8,128)(2,1)S(1)} %all-to-all-done.same_ref, bf16[16,8,1024]{2,1,0:T(8,128)(2,1)S(1)} %collective-permute-done.1.other_ref, ...), custom_call_target="tpu_custom_call" | custom-call | flops 402653184 | bytes 2359296 | tf_op jit(solution)/shard_map/outer/pallas_call | solution.py:242
  (3 shorter events, 0.0 us)
Async XLA Ops:
  1.5 19.0 %all-to-all-start = ((bf16[16,8,1024]{2,1,0:T(8,128)(2,1)}), bf16[16,8,1024]{2,1,0:T(8,128)(2,1)S(1)}, u32[]{:S(2)}, u32[]{:S(2)}) async-start(bf16[16,8,1024]{2,1,0:T(8,128)(2,1)} %broadcast_in_dim.36), calls=%async_computation | async-start | bytes 524288 | tf_op jit(solution)/shard_map/all_to_all | solution.py:186
  11.8 9.8 %collective-permute-start.2 = (bf16[272,512]{1,0:T(8,128)(2,1)S(1)}, bf16[272,512]{1,0:T(8,128)(2,1)S(1)}, u32[]{:S(2)}, u32[]{:S(2)}) collective-permute-start(bf16[272,512]{1,0:T(8,128)(2,1)S(1)} %get-tuple-element.27.near_sent_ref), channel_id=1, source_target_pairs={{0,1},{1,0},{2,3},{3,2},{4,5},{5,4},{6,7},{7,6},{8,9},{9,8},{10,11... | collective-permute-start | bytes 835592 | tf_op jit(solution)/shard_map/ppermute | solution.py:207
  11.8 14.9 %collective-permute-start = (bf16[272,512]{1,0:T(8,128)(2,1)S(1)}, bf16[272,512]{1,0:T(8,128)(2,1)S(1)}, u32[]{:S(2)}, u32[]{:S(2)}) collective-permute-start(bf16[272,512]{1,0:T(8,128)(2,1)S(1)} %get-tuple-element.28.far_sent_ref), channel_id=1, source_target_pairs={{1,2},{3,4},{5,6},{7,8},{9,10},{11,12},{13,14},{15,16},{17,18},{19... | collective-permute-start | bytes 835592 | tf_op jit(solution)/shard_map/ppermute | solution.py:206
  20.5 1.5 %collective-permute-start.1 = (bf16[16,8,1024]{2,1,0:T(8,128)(2,1)S(1)}, bf16[16,8,1024]{2,1,0:T(8,128)(2,1)S(1)}, u32[]{:S(2)}, u32[]{:S(2)}) collective-permute-start(bf16[16,8,1024]{2,1,0:T(8,128)(2,1)S(1)} %all-to-all-done.same_ref), channel_id=1, source_target_pairs={{0,1},{1,0},{2,3},{3,2},{4,5},{5,4},{6,7},{7,6},{8,9},{9,8},{10,11... | collective-permute-start | bytes 786440 | tf_op jit(solution)/shard_map/ppermute | solution.py:208

commit v2 on v0

--- a/solution.py
+++ b/solution.py
@@ -69,20 +69,21 @@
         pieces = []
         for t, bias in enumerate(biases):
             piece = scores[t * lon : (t + 1) * lon] * scale + bias
-            top = jnp.max(piece, axis=1, keepdims=True)
+            top = jnp.max(piece.astype(jnp.bfloat16), axis=1, keepdims=True).astype(jnp.float32)
             pieces.append(jnp.exp2(piece - top).astype(jnp.bfloat16))
         return jnp.concatenate(pieces, axis=0)
 
     groups = HEADS // PAIR
-    ahead = scores_of(0)
+    scores = [scores_of(group) for group in range(groups)]
+    weights = [
+        jnp.concatenate([weights_of(part) for part in scores[group]], axis=1) for group in range(groups)
+    ]
     for group in range(groups):
-        scores, ahead = ahead, scores_of(group + 1) if group + 1 < groups else None
         values = both_cores(same_ref, other_ref, columns(groups + group))
         value_parts = jnp.concatenate(
             [jnp.concatenate([values * one, one], axis=1) for one in ones], axis=0
         )
-        weights = jnp.concatenate([weights_of(part) for part in scores], axis=1)
-        both = jnp.dot(weights, value_parts, preferred_element_type=jnp.float32)
+        both = jnp.dot(weights[group], value_parts, preferred_element_type=jnp.float32)
         mixed_ref[:, columns(group)] = (both[:, :pair] / both[:, pair:]).astype(jnp.bfloat16)
 
     depth = width // len(weight_refs)
@@ -109,7 +110,10 @@
 ):
     core = meta_ref[0]
     copies = [
-        pltpu.make_async_copy(conv_hbm.at[source], conv_ref.at[i], sems.at[i])
+        pltpu.make_async_copy(
+            conv_hbm.at[source, lon_off], conv_ref.at[i, lon_off], sems.at[3 * lon_off + i]
+        )
+        for lon_off in range(3)
         for i, source in enumerate((1, 2 - 2 * core, 2 * core))
     ]
     for copy in copies:
@@ -125,11 +129,11 @@
         same_ref, other_ref, (upper_ref, lower_ref), mixed_ref,
     )
     field_ref[...] = normed.astype(jnp.bfloat16)
-    for copy in copies:
-        copy.wait()
     inputs = jnp.concatenate([field_ref[lon:, :], field_ref[: 2 * lon, :]], axis=1)
     full, open_end = [], []
     for lon_off in range(3):
+        for copy in copies[3 * lon_off : 3 * lon_off + 3]:
+            copy.wait()
         taps = conv_ref[:2, lon_off].reshape(2 * width, width)
         term = jnp.dot(inputs, taps, preferred_element_type=jnp.float32)
         full.append(
@@ -226,7 +230,7 @@
             pltpu.VMEM(conv_weight.shape, jnp.bfloat16),
             pltpu.VMEM((3 * lon, width), jnp.bfloat16),
             pltpu.VMEM((3 * lon, width), jnp.bfloat16),
-            pltpu.SemaphoreType.DMA((3,)),
+            pltpu.SemaphoreType.DMA((9,)),
         ],
         compiler_params=params,
         cost_estimate=pl.CostEstimate(

time: 30.9 us -> 31 us (level)
  transfers between devices with their start and end apart: 4 -> 4, of which waited for: 2 -> 2; matrix products, arithmetic and copies ran while one was open for 10% -> 10% of each run, Pallas kernels for 15% -> 16%
where the time goes in v2:
time: 31 us; the launch traced here: 30.6 us
  starting transfers between devices  9.06 us (29%)
  Pallas kernels  8.56 us (28%)
  waiting for transfers between devices  8.3 us (27%)
  local copies, waits for them, and re-layouts  2.97 us (10%)
  other arithmetic  1.58 us (5%)
    all_to_all x1, starting transfers between devices, on_device(): lax.all_to_all(jnp.broadcast_to(block[None], (pairs,) + block.shape), AXE...  8.31 us
    all_to_all x1, waiting for transfers between devices, on_device(): lax.all_to_all(jnp.broadcast_to(block[None], (pairs,) + block.shape), AXE...  7.91 us
    pallas_call x1, Pallas kernels, on_device(): pl.pallas_call(functools.partial(inner_kernel, *sizes), out_shape=[jax.Sh...  4.78 us
    pallas_call x1, Pallas kernels, on_device(): pl.pallas_call(functools.partial(outer_kernel, *sizes), out_shape=jax.Sha...  3.78 us
    split x1, local copies, waits for them, and re-layouts, on_device(): jnp.split(grid_feat, tiles, axis=0)  1.13 us
    split x1, local copies, waits for them, and re-layouts, on_device(): jnp.split(out_weight, 2, axis=0)  1.06 us
    broadcast_in_dim x1, local copies, waits for them, and re-layouts, on_device(): jnp.broadcast_to(block[None], (pairs,) + block.shape)  0.73 us
    concatenate x1, other arithmetic, on_device(): block = jnp.concatenate([obs_keys, obs_values], axis=1)  0.72 us
  transfers between devices with their start and end apart: 4, of which 2 were waited for; matrix products, arithmetic and copies ran while one was open for 10% of the time, Pallas kernels for 16%

profile of v2, /device:TPU:0, one launch (start us, length us, event | category | flops | bytes accessed | tf_op | source)
XLA Modules:
  0.0 30.6 jit_solution(14044886007726961410)
XLA Ops:
  0.0 0.7 %pad_maximum_fusion.2 = bf16[8,1024]{1,0:T(8,128)(2,1)S(1)} fusion(bf16[8,512]{1,0:T(8,128)(2,1)} %param.11, bf16[8,512]{1,0:T(8,128)(2,1)} %param.10), kind=kLoop, calls=%fused_computation.4 | loop fusion | flops 32768 | bytes 32768 | tf_op jit(solution)/shard_map/concatenate | solution.py:183
  0.7 0.7 %broadcast_in_dim.36 = bf16[16,8,1024]{2,1,0:T(8,128)(2,1)} broadcast(bf16[8,1024]{1,0:T(8,128)(2,1)S(1)} %pad_maximum_fusion.2), dimensions={1,2} | broadcast | bytes 278528 | tf_op jit(solution)/shard_map/broadcast_in_dim | solution.py:186
  1.5 8.3 %all-to-all-start = ((bf16[16,8,1024]{2,1,0:T(8,128)(2,1)}), bf16[16,8,1024]{2,1,0:T(8,128)(2,1)S(1)}, u32[]{:S(2)}, u32[]{:S(2)}) async-start(bf16[16,8,1024]{2,1,0:T(8,128)(2,1)} %broadcast_in_dim.36), calls=%async_computation | async-start | bytes 524288 | tf_op jit(solution)/shard_map/all_to_all | solution.py:185
  9.8 1.1 %fusion.2 = (bf16[128,512]{1,0:T(8,128)(2,1)S(1)}, bf16[128,512]{1,0:T(8,128)(2,1)S(1)}, bf16[128,512]{1,0:T(8,128)(2,1)S(1)}, bf16[128,512]{1,0:T(8,128)(2,1)S(1)}) fusion(bf16[256,512]{1,0:T(8,128)(2,1)} %param.8, bf16[256,512]{1,0:T(8,128)(2,1)} %param.9), kind=kLoop, calls=%fused_computation.11 | loop fusion | bytes 1048576 | tf_op jit(solution)/shard_map/split | solution.py:193
  10.9 0.7 %fusion = bf16[2,2]{1,0:T(2,128)(2,1)S(1)} fusion(s32[2,2]{1,0:T(2,128)} %param.12, s32[2]{0:T(128)} %param.13), kind=kLoop, calls=%fused_computation.8 | loop fusion | flops 12 | bytes 32 | tf_op jit(solution)/shard_map/convert_element_type | solution.py:195
  11.7 0.1 broadcast_select_fusion
  11.8 0.1 collective-permute-start.2
  11.8 0.7 %collective-permute-start = (bf16[272,512]{1,0:T(8,128)(2,1)S(1)}, bf16[272,512]{1,0:T(8,128)(2,1)S(1)}, u32[]{:S(2)}, u32[]{:S(2)}) collective-permute-start(bf16[272,512]{1,0:T(8,128)(2,1)S(1)} %get-tuple-element.28.far_sent_ref), channel_id=1, source_target_pairs={{1,2},{3,4},{5,6},{7,8},{9,10},{11,12},{13,14},{15,16},{17,18},{19... | collective-permute-start | bytes 835592 | tf_op jit(solution)/shard_map/ppermute | solution.py:205
  12.5 7.9 %all-to-all-done.same_ref = bf16[16,8,1024]{2,1,0:T(8,128)(2,1)S(1)} async-done(((bf16[16,8,1024]{2,1,0:T(8,128)(2,1)}), bf16[16,8,1024]{2,1,0:T(8,128)(2,1)S(1)}, u32[]{:S(2)}, u32[]{:S(2)}) %all-to-all-start) | async-done | bytes 262176 | tf_op jit(solution)/shard_map/all_to_all | solution.py:185
  20.5 0.0 collective-permute-start.1
  20.5 0.1 pad_add_fusion.meta_ref
  20.5 1.1 %fusion.1 = (bf16[256,512]{1,0:T(8,128)(2,1)S(1)}, bf16[256,512]{1,0:T(8,128)(2,1)S(1)}) fusion(bf16[512,512]{1,0:T(8,128)(2,1)} %param.14), kind=kLoop, calls=%fused_computation.10 | loop fusion | bytes 1048576 | tf_op jit(solution)/shard_map/split | solution.py:209
  21.6 0.0 collective-permute-done.2.near_ref
  21.6 0.4 %collective-permute-done.1.other_ref = bf16[16,8,1024]{2,1,0:T(8,128)(2,1)S(1)} collective-permute-done((bf16[16,8,1024]{2,1,0:T(8,128)(2,1)S(1)}, bf16[16,8,1024]{2,1,0:T(8,128)(2,1)S(1)}, u32[]{:S(2)}, u32[]{:S(2)}) %collective-permute-start.1) | collective-permute-done | bytes 262176 | tf_op jit(solution)/shard_map/ppermute | solution.py:207
  22.0 4.8 %inner.1 = (bf16[128,512]{1,0:T(8,128)(2,1)S(1)}, f32[128,512]{1,0:T(8,128)S(1)}, bf16[512,256]{1,0:T(8,128)(2,1)S(1)}) custom-call(s32[2]{0:T(128)S(1)} %pad_add_fusion.meta_ref, bf16[272,512]{1,0:T(8,128)(2,1)S(1)} %collective-permute-done.2.near_ref, bf16[272,512]{1,0:T(8,128)(2,1)S(1)} %get-tuple-element.27.near_sent_ref, ...), custom_call_target="tpu_custom_call" | custom-call | flops 1610612736 | bytes 4718592 | tf_op jit(solution)/shard_map/inner/pallas_call | solution.py:220
  26.8 0.0 collective-permute-done.far_ref
  26.8 3.8 %outer.1 = bf16[256,512]{1,0:T(8,128)(2,1)} custom-call(s32[2]{0:T(128)S(1)} %pad_add_fusion.meta_ref, bf16[272,512]{1,0:T(8,128)(2,1)S(1)} %collective-permute-done.far_ref, bf16[16,8,1024]{2,1,0:T(8,128)(2,1)S(1)} %all-to-all-done.same_ref, bf16[16,8,1024]{2,1,0:T(8,128)(2,1)S(1)} %collective-permute-done.1.other_ref, ...), custom_call_target="tpu_custom_call" | custom-call | flops 402653184 | bytes 2359296 | tf_op jit(solution)/shard_map/outer/pallas_call | solution.py:241
  (3 shorter events, 0.0 us)
Async XLA Ops:
  1.5 19.0 %all-to-all-start = ((bf16[16,8,1024]{2,1,0:T(8,128)(2,1)}), bf16[16,8,1024]{2,1,0:T(8,128)(2,1)S(1)}, u32[]{:S(2)}, u32[]{:S(2)}) async-start(bf16[16,8,1024]{2,1,0:T(8,128)(2,1)} %broadcast_in_dim.36), calls=%async_computation | async-start | bytes 524288 | tf_op jit(solution)/shard_map/all_to_all | solution.py:185
  11.8 9.8 %collective-permute-start.2 = (bf16[272,512]{1,0:T(8,128)(2,1)S(1)}, bf16[272,512]{1,0:T(8,128)(2,1)S(1)}, u32[]{:S(2)}, u32[]{:S(2)}) collective-permute-start(bf16[272,512]{1,0:T(8,128)(2,1)S(1)} %get-tuple-element.27.near_sent_ref), channel_id=1, source_target_pairs={{0,1},{1,0},{2,3},{3,2},{4,5},{5,4},{6,7},{7,6},{8,9},{9,8},{10,11... | collective-permute-start | bytes 835592 | tf_op jit(solution)/shard_map/ppermute | solution.py:206
  11.8 14.9 %collective-permute-start = (bf16[272,512]{1,0:T(8,128)(2,1)S(1)}, bf16[272,512]{1,0:T(8,128)(2,1)S(1)}, u32[]{:S(2)}, u32[]{:S(2)}) collective-permute-start(bf16[272,512]{1,0:T(8,128)(2,1)S(1)} %get-tuple-element.28.far_sent_ref), channel_id=1, source_target_pairs={{1,2},{3,4},{5,6},{7,8},{9,10},{11,12},{13,14},{15,16},{17,18},{19... | collective-permute-start | bytes 835592 | tf_op jit(solution)/shard_map/ppermute | solution.py:205
  20.5 1.5 %collective-permute-start.1 = (bf16[16,8,1024]{2,1,0:T(8,128)(2,1)S(1)}, bf16[16,8,1024]{2,1,0:T(8,128)(2,1)S(1)}, u32[]{:S(2)}, u32[]{:S(2)}) collective-permute-start(bf16[16,8,1024]{2,1,0:T(8,128)(2,1)S(1)} %all-to-all-done.same_ref), channel_id=1, source_target_pairs={{0,1},{1,0},{2,3},{3,2},{4,5},{5,4},{6,7},{7,6},{8,9},{9,8},{10,11... | collective-permute-start | bytes 786440 | tf_op jit(solution)/shard_map/ppermute | solution.py:207

commit v3 on v2

--- a/solution.py
+++ b/solution.py
@@ -69,7 +69,7 @@
         pieces = []
         for t, bias in enumerate(biases):
             piece = scores[t * lon : (t + 1) * lon] * scale + bias
-            top = jnp.max(piece.astype(jnp.bfloat16), axis=1, keepdims=True).astype(jnp.float32)
+            top = jnp.max(piece, axis=1, keepdims=True)
             pieces.append(jnp.exp2(piece - top).astype(jnp.bfloat16))
         return jnp.concatenate(pieces, axis=0)
 
@@ -106,15 +106,15 @@
 def inner_kernel(
     lon, width, nblocks, rows,
     meta_ref, near_ref, near_sent_ref, far_sent_ref, same_ref, other_ref, upper_ref, lower_ref,
-    conv_hbm, done_ref, partial_ref, keys_ref, conv_ref, mixed_ref, field_ref, sems,
+    conv_hbm, edge_ref, partial_ref, keys_ref, conv_ref, mixed_ref, field_ref, sems,
 ):
     core = meta_ref[0]
     copies = [
         pltpu.make_async_copy(
-            conv_hbm.at[source, lon_off], conv_ref.at[i, lon_off], sems.at[3 * lon_off + i]
+            conv_hbm.at[source, lon_off], conv_ref.at[i, lon_off], sems.at[2 * lon_off + i]
         )
         for lon_off in range(3)
-        for i, source in enumerate((1, 2 - 2 * core, 2 * core))
+        for i, source in enumerate((1, 2 - 2 * core))
     ]
     for copy in copies:
         copy.start()
@@ -129,25 +129,23 @@
         same_ref, other_ref, (upper_ref, lower_ref), mixed_ref,
     )
     field_ref[...] = normed.astype(jnp.bfloat16)
+    edge_ref[...] = field_ref[2 * lon :, :]
     inputs = jnp.concatenate([field_ref[lon:, :], field_ref[: 2 * lon, :]], axis=1)
-    full, open_end = [], []
+    terms = []
     for lon_off in range(3):
-        for copy in copies[3 * lon_off : 3 * lon_off + 3]:
+        for copy in copies[2 * lon_off : 2 * lon_off + 2]:
             copy.wait()
-        taps = conv_ref[:2, lon_off].reshape(2 * width, width)
-        term = jnp.dot(inputs, taps, preferred_element_type=jnp.float32)
-        full.append(
-            term[:lon]
-            + jnp.dot(field_ref[2 * lon :, :], conv_ref[2, lon_off], preferred_element_type=jnp.float32)
-        )
-        open_end.append(term[lon:])
-    done_ref[...] = (wide[lon : 2 * lon] + around(full, lon)).astype(jnp.bfloat16)
-    partial_ref[...] = wide[2 * lon :] + around(open_end, lon)
+        taps = conv_ref[:, lon_off].reshape(2 * width, width)
+        terms.append(jnp.dot(inputs, taps, preferred_element_type=jnp.float32))
+    for start in (0, lon):
+        here = slice(start, start + lon)
+        shifted = around([term[here] for term in terms], lon)
+        partial_ref[here, :] = wide[start + lon : start + 2 * lon] + shifted
 
 
 def outer_kernel(
     lon, width, nblocks, rows,
-    meta_ref, far_ref, same_ref, other_ref, upper_ref, lower_ref, done_ref, partial_ref, keys_ref,
+    meta_ref, far_ref, same_ref, other_ref, upper_ref, lower_ref, edge_ref, partial_ref, keys_ref,
     conv_hbm, out_ref, conv_ref, mixed_ref, sem,
 ):
     core = meta_ref[0]
@@ -157,14 +155,16 @@
         lon, width, nblocks, rows, core, (far_ref,), lambda cols: keys_ref[cols, :],
         same_ref, other_ref, (upper_ref, lower_ref), mixed_ref,
     )
-    field = jnp.where(meta_ref[1] > 0, normed, 0.0).astype(jnp.bfloat16)
+    far = jnp.where(meta_ref[1] > 0, normed, 0.0).astype(jnp.bfloat16)
+    field = jnp.concatenate([edge_ref[...], far], axis=0)
     copy.wait()
-    parts = [
+    terms = [
         jnp.dot(field, conv_ref[lon_off], preferred_element_type=jnp.float32) for lon_off in range(3)
     ]
-    last = (partial_ref[...] + around(parts, lon)).astype(jnp.bfloat16)
-    out_ref[pl.ds(pl.multiple_of((1 - core) * lon, lon), lon), :] = done_ref[...]
-    out_ref[pl.ds(pl.multiple_of(core * lon, lon), lon), :] = last
+    for start, tile in ((0, 1 - core), (lon, core)):
+        here = slice(start, start + lon)
+        total = partial_ref[here, :] + around([term[here] for term in terms], lon)
+        out_ref[pl.ds(pl.multiple_of(tile * lon, lon), lon), :] = total.astype(jnp.bfloat16)
 
 
 def on_device(
@@ -217,24 +217,24 @@
     sizes = (lon, width, nblocks, rows)
     params = pltpu.CompilerParams(vmem_limit_bytes=48 * 2**20)
     tap_flops, row_flops = 2 * lon * width * width, 2 * lon * width * (width + 4 * obs)
-    done, partial, keys = pl.pallas_call(
+    edge, partial, keys = pl.pallas_call(
         functools.partial(inner_kernel, *sizes),
         out_shape=[
             jax.ShapeDtypeStruct((lon, width), jnp.bfloat16),
-            jax.ShapeDtypeStruct((lon, width), jnp.float32),
+            jax.ShapeDtypeStruct((q_dev, width), jnp.float32),
             jax.ShapeDtypeStruct((width, obs), jnp.bfloat16),
         ],
         in_specs=[smem] + [vmem] * 7 + [hbm],
         out_specs=[vmem] * 3,
         scratch_shapes=[
-            pltpu.VMEM(conv_weight.shape, jnp.bfloat16),
+            pltpu.VMEM((2,) + conv_weight.shape[1:], jnp.bfloat16),
             pltpu.VMEM((3 * lon, width), jnp.bfloat16),
             pltpu.VMEM((3 * lon, width), jnp.bfloat16),
-            pltpu.SemaphoreType.DMA((9,)),
+            pltpu.SemaphoreType.DMA((6,)),
         ],
         compiler_params=params,
         cost_estimate=pl.CostEstimate(
-            flops=3 * row_flops + 15 * tap_flops, bytes_accessed=2 * conv_weight.size, transcendentals=0
+            flops=3 * row_flops + 12 * tap_flops, bytes_accessed=2 * conv_weight.size, transcendentals=0
         ),
         name="inner",
     )(meta, near, near_sent, far_sent, same, other, upper, lower, conv_weight)
@@ -250,10 +250,10 @@
         ],
         compiler_params=params,
         cost_estimate=pl.CostEstimate(
-            flops=row_flops + 3 * tap_flops, bytes_accessed=conv_weight.size, transcendentals=0
+            flops=row_flops + 6 * tap_flops, bytes_accessed=conv_weight.size, transcendentals=0
         ),
         name="outer",
-    )(meta, far, same, other, upper, lower, done, partial, keys, conv_weight)
+    )(meta, far, same, other, upper, lower, edge, partial, keys, conv_weight)
 
 
 def solution(mesh):

time: 31 us -> 30 us (0.968)
  Pallas kernels: 8.56 us -> 7.65 us
    pallas_call x1, Pallas kernels: 4.78 us -> 4.02 us  [on_device(): pl.pallas_call(functools.partial(inner_kernel, *sizes), out_shape=[jax.Sh...]
  transfers between devices with their start and end apart: 4 -> 4, of which waited for: 2 -> 2; matrix products, arithmetic and copies ran while one was open for 10% -> 10% of each run, Pallas kernels for 16% -> 14%
where the time goes in v3:
time: 30 us; the launch traced here: 29.7 us
  starting transfers between devices  9.06 us (30%)
  waiting for transfers between devices  8.3 us (28%)
  Pallas kernels  7.65 us (26%)
  local copies, waits for them, and re-layouts  2.97 us (10%)
  other arithmetic  1.58 us (5%)
    all_to_all x1, starting transfers between devices, on_device(): lax.all_to_all(jnp.broadcast_to(block[None], (pairs,) + block.shape), AXE...  8.31 us
    all_to_all x1, waiting for transfers between devices, on_device(): lax.all_to_all(jnp.broadcast_to(block[None], (pairs,) + block.shape), AXE...  7.91 us
    pallas_call x1, Pallas kernels, on_device(): pl.pallas_call(functools.partial(inner_kernel, *sizes), out_shape=[jax.Sh...  4.02 us
    pallas_call x1, Pallas kernels, on_device(): pl.pallas_call(functools.partial(outer_kernel, *sizes), out_shape=jax.Sha...  3.63 us
    split x1, local copies, waits for them, and re-layouts, on_device(): jnp.split(grid_feat, tiles, axis=0)  1.13 us
    split x1, local copies, waits for them, and re-layouts, on_device(): jnp.split(out_weight, 2, axis=0)  1.06 us
    broadcast_in_dim x1, local copies, waits for them, and re-layouts, on_device(): jnp.broadcast_to(block[None], (pairs,) + block.shape)  0.73 us
    concatenate x1, other arithmetic, on_device(): block = jnp.concatenate([obs_keys, obs_values], axis=1)  0.72 us
  transfers between devices with their start and end apart: 4, of which 2 were waited for; matrix products, arithmetic and copies ran while one was open for 10% of the time, Pallas kernels for 14%

profile of v3, /device:TPU:0, one launch (start us, length us, event | category | flops | bytes accessed | tf_op | source)
XLA Modules:
  0.0 29.7 jit_solution(17123195782400175653)
XLA Ops:
  0.0 0.7 %pad_maximum_fusion.2 = bf16[8,1024]{1,0:T(8,128)(2,1)S(1)} fusion(bf16[8,512]{1,0:T(8,128)(2,1)} %param.11, bf16[8,512]{1,0:T(8,128)(2,1)} %param.10), kind=kLoop, calls=%fused_computation.4 | loop fusion | flops 32768 | bytes 32768 | tf_op jit(solution)/shard_map/concatenate | solution.py:183
  0.7 0.7 %broadcast_in_dim.36 = bf16[16,8,1024]{2,1,0:T(8,128)(2,1)} broadcast(bf16[8,1024]{1,0:T(8,128)(2,1)S(1)} %pad_maximum_fusion.2), dimensions={1,2} | broadcast | bytes 278528 | tf_op jit(solution)/shard_map/broadcast_in_dim | solution.py:186
  1.5 8.3 %all-to-all-start = ((bf16[16,8,1024]{2,1,0:T(8,128)(2,1)}), bf16[16,8,1024]{2,1,0:T(8,128)(2,1)S(1)}, u32[]{:S(2)}, u32[]{:S(2)}) async-start(bf16[16,8,1024]{2,1,0:T(8,128)(2,1)} %broadcast_in_dim.36), calls=%async_computation | async-start | bytes 524288 | tf_op jit(solution)/shard_map/all_to_all | solution.py:185
  9.8 1.1 %fusion.2 = (bf16[128,512]{1,0:T(8,128)(2,1)S(1)}, bf16[128,512]{1,0:T(8,128)(2,1)S(1)}, bf16[128,512]{1,0:T(8,128)(2,1)S(1)}, bf16[128,512]{1,0:T(8,128)(2,1)S(1)}) fusion(bf16[256,512]{1,0:T(8,128)(2,1)} %param.8, bf16[256,512]{1,0:T(8,128)(2,1)} %param.9), kind=kLoop, calls=%fused_computation.11 | loop fusion | bytes 1048576 | tf_op jit(solution)/shard_map/split | solution.py:193
  10.9 0.7 %fusion = bf16[2,2]{1,0:T(2,128)(2,1)S(1)} fusion(s32[2,2]{1,0:T(2,128)} %param.12, s32[2]{0:T(128)} %param.13), kind=kLoop, calls=%fused_computation.8 | loop fusion | flops 12 | bytes 32 | tf_op jit(solution)/shard_map/convert_element_type | solution.py:195
  11.7 0.1 broadcast_select_fusion
  11.8 0.1 collective-permute-start.2
  11.8 0.7 %collective-permute-start = (bf16[272,512]{1,0:T(8,128)(2,1)S(1)}, bf16[272,512]{1,0:T(8,128)(2,1)S(1)}, u32[]{:S(2)}, u32[]{:S(2)}) collective-permute-start(bf16[272,512]{1,0:T(8,128)(2,1)S(1)} %get-tuple-element.28.far_sent_ref), channel_id=1, source_target_pairs={{1,2},{3,4},{5,6},{7,8},{9,10},{11,12},{13,14},{15,16},{17,18},{19... | collective-permute-start | bytes 835592 | tf_op jit(solution)/shard_map/ppermute | solution.py:205
  12.5 7.9 %all-to-all-done.same_ref = bf16[16,8,1024]{2,1,0:T(8,128)(2,1)S(1)} async-done(((bf16[16,8,1024]{2,1,0:T(8,128)(2,1)}), bf16[16,8,1024]{2,1,0:T(8,128)(2,1)S(1)}, u32[]{:S(2)}, u32[]{:S(2)}) %all-to-all-start) | async-done | bytes 262176 | tf_op jit(solution)/shard_map/all_to_all | solution.py:185
  20.5 0.0 collective-permute-start.1
  20.5 0.1 pad_add_fusion.meta_ref
  20.5 1.1 %fusion.1 = (bf16[256,512]{1,0:T(8,128)(2,1)S(1)}, bf16[256,512]{1,0:T(8,128)(2,1)S(1)}) fusion(bf16[512,512]{1,0:T(8,128)(2,1)} %param.14), kind=kLoop, calls=%fused_computation.10 | loop fusion | bytes 1048576 | tf_op jit(solution)/shard_map/split | solution.py:209
  21.6 0.0 collective-permute-done.2.near_ref
  21.6 0.4 %collective-permute-done.1.other_ref = bf16[16,8,1024]{2,1,0:T(8,128)(2,1)S(1)} collective-permute-done((bf16[16,8,1024]{2,1,0:T(8,128)(2,1)S(1)}, bf16[16,8,1024]{2,1,0:T(8,128)(2,1)S(1)}, u32[]{:S(2)}, u32[]{:S(2)}) %collective-permute-start.1) | collective-permute-done | bytes 262176 | tf_op jit(solution)/shard_map/ppermute | solution.py:207
  22.0 4.0 %inner.1 = (bf16[128,512]{1,0:T(8,128)(2,1)S(1)}, f32[256,512]{1,0:T(8,128)S(1)}, bf16[512,256]{1,0:T(8,128)(2,1)S(1)}) custom-call(s32[2]{0:T(128)S(1)} %pad_add_fusion.meta_ref, bf16[272,512]{1,0:T(8,128)(2,1)S(1)} %collective-permute-done.2.near_ref, bf16[272,512]{1,0:T(8,128)(2,1)S(1)} %get-tuple-element.27.near_sent_ref, ...), custom_call_target="tpu_custom_call" | custom-call | flops 1409286144 | bytes 4718592 | tf_op jit(solution)/shard_map/inner/pallas_call | solution.py:220
  26.0 0.0 collective-permute-done.far_ref
  26.0 3.6 %outer.1 = bf16[256,512]{1,0:T(8,128)(2,1)} custom-call(s32[2]{0:T(128)S(1)} %pad_add_fusion.meta_ref, bf16[272,512]{1,0:T(8,128)(2,1)S(1)} %collective-permute-done.far_ref, bf16[16,8,1024]{2,1,0:T(8,128)(2,1)S(1)} %all-to-all-done.same_ref, bf16[16,8,1024]{2,1,0:T(8,128)(2,1)S(1)} %collective-permute-done.1.other_ref, ...), custom_call_target="tpu_custom_call" | custom-call | flops 603979776 | bytes 2359296 | tf_op jit(solution)/shard_map/outer/pallas_call | solution.py:241
  (3 shorter events, 0.0 us)
Async XLA Ops:
  1.5 19.0 %all-to-all-start = ((bf16[16,8,1024]{2,1,0:T(8,128)(2,1)}), bf16[16,8,1024]{2,1,0:T(8,128)(2,1)S(1)}, u32[]{:S(2)}, u32[]{:S(2)}) async-start(bf16[16,8,1024]{2,1,0:T(8,128)(2,1)} %broadcast_in_dim.36), calls=%async_computation | async-start | bytes 524288 | tf_op jit(solution)/shard_map/all_to_all | solution.py:185
  11.8 9.8 %collective-permute-start.2 = (bf16[272,512]{1,0:T(8,128)(2,1)S(1)}, bf16[272,512]{1,0:T(8,128)(2,1)S(1)}, u32[]{:S(2)}, u32[]{:S(2)}) collective-permute-start(bf16[272,512]{1,0:T(8,128)(2,1)S(1)} %get-tuple-element.27.near_sent_ref), channel_id=1, source_target_pairs={{0,1},{1,0},{2,3},{3,2},{4,5},{5,4},{6,7},{7,6},{8,9},{9,8},{10,11... | collective-permute-start | bytes 835592 | tf_op jit(solution)/shard_map/ppermute | solution.py:206
  11.8 14.2 %collective-permute-start = (bf16[272,512]{1,0:T(8,128)(2,1)S(1)}, bf16[272,512]{1,0:T(8,128)(2,1)S(1)}, u32[]{:S(2)}, u32[]{:S(2)}) collective-permute-start(bf16[272,512]{1,0:T(8,128)(2,1)S(1)} %get-tuple-element.28.far_sent_ref), channel_id=1, source_target_pairs={{1,2},{3,4},{5,6},{7,8},{9,10},{11,12},{13,14},{15,16},{17,18},{19... | collective-permute-start | bytes 835592 | tf_op jit(solution)/shard_map/ppermute | solution.py:205
  20.5 1.5 %collective-permute-start.1 = (bf16[16,8,1024]{2,1,0:T(8,128)(2,1)S(1)}, bf16[16,8,1024]{2,1,0:T(8,128)(2,1)S(1)}, u32[]{:S(2)}, u32[]{:S(2)}) collective-permute-start(bf16[16,8,1024]{2,1,0:T(8,128)(2,1)S(1)} %all-to-all-done.same_ref), channel_id=1, source_target_pairs={{0,1},{1,0},{2,3},{3,2},{4,5},{5,4},{6,7},{7,6},{8,9},{9,8},{10,11... | collective-permute-start | bytes 786440 | tf_op jit(solution)/shard_map/ppermute | solution.py:207

commit v4 on v3

--- a/solution.py
+++ b/solution.py
@@ -16,9 +16,10 @@
 LIMIT_ROWS = 16
 
 
-def both_cores(same_ref, other_ref, cols):
+def both_cores(same_ref, other_ref, kind, cols):
     return jnp.concatenate(
-        [ref[:, :, cols].reshape(-1, cols.stop - cols.start) for ref in (same_ref, other_ref)], axis=0
+        [ref[:, kind, :, cols].reshape(-1, cols.stop - cols.start) for ref in (same_ref, other_ref)],
+        axis=0,
     )
 
 
@@ -79,7 +80,7 @@
         jnp.concatenate([weights_of(part) for part in scores[group]], axis=1) for group in range(groups)
     ]
     for group in range(groups):
-        values = both_cores(same_ref, other_ref, columns(groups + group))
+        values = both_cores(same_ref, other_ref, 1, columns(group))
         value_parts = jnp.concatenate(
             [jnp.concatenate([values * one, one], axis=1) for one in ones], axis=0
         )
@@ -106,7 +107,7 @@
 def inner_kernel(
     lon, width, nblocks, rows,
     meta_ref, near_ref, near_sent_ref, far_sent_ref, same_ref, other_ref, upper_ref, lower_ref,
-    conv_hbm, edge_ref, partial_ref, keys_ref, conv_ref, mixed_ref, field_ref, sems,
+    conv_hbm, edge_ref, partial_ref, keys_ref, last_ref, conv_ref, mixed_ref, field_ref, sems,
 ):
     core = meta_ref[0]
     copies = [
@@ -116,11 +117,12 @@
         for lon_off in range(3)
         for i, source in enumerate((1, 2 - 2 * core))
     ]
+    copies.append(pltpu.make_async_copy(conv_hbm.at[2 * core], last_ref, sems.at[6]))
     for copy in copies:
         copy.start()
 
     def keys_of(cols):
-        keys = both_cores(same_ref, other_ref, cols).T
+        keys = both_cores(same_ref, other_ref, 0, cols).T
         keys_ref[cols, :] = keys
         return keys
 
@@ -141,23 +143,21 @@
         here = slice(start, start + lon)
         shifted = around([term[here] for term in terms], lon)
         partial_ref[here, :] = wide[start + lon : start + 2 * lon] + shifted
+    copies[6].wait()
 
 
 def outer_kernel(
     lon, width, nblocks, rows,
     meta_ref, far_ref, same_ref, other_ref, upper_ref, lower_ref, edge_ref, partial_ref, keys_ref,
-    conv_hbm, out_ref, conv_ref, mixed_ref, sem,
+    conv_ref, out_ref, mixed_ref,
 ):
     core = meta_ref[0]
-    copy = pltpu.make_async_copy(conv_hbm.at[2 * core], conv_ref, sem)
-    copy.start()
     _, normed = attend(
         lon, width, nblocks, rows, core, (far_ref,), lambda cols: keys_ref[cols, :],
         same_ref, other_ref, (upper_ref, lower_ref), mixed_ref,
     )
     far = jnp.where(meta_ref[1] > 0, normed, 0.0).astype(jnp.bfloat16)
     field = jnp.concatenate([edge_ref[...], far], axis=0)
-    copy.wait()
     terms = [
         jnp.dot(field, conv_ref[lon_off], preferred_element_type=jnp.float32) for lon_off in range(3)
     ]
@@ -180,11 +180,11 @@
     me = lax.axis_index(AXES)
     core = me % CORES
 
-    block = jnp.concatenate([obs_keys, obs_values], axis=1)
     groups = [list(range(c, devices, CORES)) for c in range(CORES)]
-    same = lax.all_to_all(
-        jnp.broadcast_to(block[None], (pairs,) + block.shape), AXES, 0, 0, axis_index_groups=groups
-    )
+    shape = (pairs, 2) + obs_keys.shape
+    is_key = lax.broadcasted_iota(jnp.int32, shape, 1) == 0
+    blocks = jnp.where(is_key, obs_keys[None, None], obs_values[None, None])
+    same = lax.all_to_all(blocks, AXES, 0, 0, axis_index_groups=groups)
     swap = [(i, i ^ 1) for i in range(devices)]
     across = [(i, i + 1) for i in range(1, devices - 1, CORES)]
     across += [(target, source) for source, target in across]
@@ -217,20 +217,21 @@
     sizes = (lon, width, nblocks, rows)
     params = pltpu.CompilerParams(vmem_limit_bytes=48 * 2**20)
     tap_flops, row_flops = 2 * lon * width * width, 2 * lon * width * (width + 4 * obs)
-    edge, partial, keys = pl.pallas_call(
+    edge, partial, keys, taps = pl.pallas_call(
         functools.partial(inner_kernel, *sizes),
         out_shape=[
             jax.ShapeDtypeStruct((lon, width), jnp.bfloat16),
             jax.ShapeDtypeStruct((q_dev, width), jnp.float32),
             jax.ShapeDtypeStruct((width, obs), jnp.bfloat16),
+            jax.ShapeDtypeStruct(conv_weight.shape[1:], jnp.bfloat16),
         ],
         in_specs=[smem] + [vmem] * 7 + [hbm],
-        out_specs=[vmem] * 3,
+        out_specs=[vmem] * 4,
         scratch_shapes=[
             pltpu.VMEM((2,) + conv_weight.shape[1:], jnp.bfloat16),
             pltpu.VMEM((3 * lon, width), jnp.bfloat16),
             pltpu.VMEM((3 * lon, width), jnp.bfloat16),
-            pltpu.SemaphoreType.DMA((6,)),
+            pltpu.SemaphoreType.DMA((7,)),
         ],
         compiler_params=params,
         cost_estimate=pl.CostEstimate(
@@ -241,19 +242,17 @@
     return pl.pallas_call(
         functools.partial(outer_kernel, *sizes),
         out_shape=jax.ShapeDtypeStruct((q_dev, width), jnp.bfloat16),
-        in_specs=[smem] + [vmem] * 8 + [hbm],
+        in_specs=[smem] + [vmem] * 9,
         out_specs=vmem,
         scratch_shapes=[
-            pltpu.VMEM(conv_weight.shape[1:], jnp.bfloat16),
             pltpu.VMEM((lon, width), jnp.bfloat16),
-            pltpu.SemaphoreType.DMA,
         ],
         compiler_params=params,
         cost_estimate=pl.CostEstimate(
             flops=row_flops + 6 * tap_flops, bytes_accessed=conv_weight.size, transcendentals=0
         ),
         name="outer",
-    )(meta, far, same, other, upper, lower, edge, partial, keys, conv_weight)
+    )(meta, far, same, other, upper, lower, edge, partial, keys, taps)
 
 
 def solution(mesh):

time: 30 us -> 29.5 us (0.983)
  other arithmetic: 1.58 us -> 2.38 us
  local copies, waits for them, and re-layouts: 2.97 us -> 2.24 us
  Pallas kernels: 7.65 us -> 7.01 us
    select_n x0 -> x1, other arithmetic: none -> 1.51 us  [on_device(): blocks = jnp.where(is_key, obs_keys[None, None], obs_values[None, None])]
    pallas_call x1, Pallas kernels: 3.63 us -> 2.63 us  [on_device(): pl.pallas_call(functools.partial(outer_kernel, *sizes), out_shape=jax.Sha...]
    broadcast_in_dim x1 -> x0, local copies, waits for them, and re-layouts: 0.73 us -> none  [on_device(): jnp.broadcast_to(block[None], (pairs,) + block.shape)]
    concatenate x1 -> x0, other arithmetic: 0.72 us -> none  [on_device(): block = jnp.concatenate([obs_keys, obs_values], axis=1)]
    pallas_call x1, Pallas kernels: 4.02 us -> 4.38 us  [on_device(): pl.pallas_call(functools.partial(inner_kernel, *sizes), out_shape=[jax.Sh...]
  transfers between devices with their start and end apart: 4 -> 4, of which waited for: 2 -> 2; matrix products, arithmetic and copies ran while one was open for 10% -> 11% of each run, Pallas kernels for 14% -> 15%
where the time goes in v4:
time: 29.5 us; the launch traced here: 29.1 us
  starting transfers between devices  9.06 us (31%)
  waiting for transfers between devices  8.3 us (28%)
  Pallas kernels  7.01 us (24%)
  other arithmetic  2.38 us (8%)
  local copies, waits for them, and re-layouts  2.24 us (8%)
    all_to_all x1, starting transfers between devices, on_device(): same = lax.all_to_all(blocks, AXES, 0, 0, axis_index_groups=groups)  8.31 us
    all_to_all x1, waiting for transfers between devices, on_device(): same = lax.all_to_all(blocks, AXES, 0, 0, axis_index_groups=groups)  7.91 us
    pallas_call x1, Pallas kernels, on_device(): pl.pallas_call(functools.partial(inner_kernel, *sizes), out_shape=[jax.Sh...  4.38 us
    pallas_call x1, Pallas kernels, on_device(): pl.pallas_call(functools.partial(outer_kernel, *sizes), out_shape=jax.Sha...  2.63 us
    select_n x1, other arithmetic, on_device(): blocks = jnp.where(is_key, obs_keys[None, None], obs_values[None, None])  1.51 us
    split x1, local copies, waits for them, and re-layouts, on_device(): jnp.split(grid_feat, tiles, axis=0)  1.13 us
    split x1, local copies, waits for them, and re-layouts, on_device(): jnp.split(out_weight, 2, axis=0)  1.06 us
    convert_element_type x1, other arithmetic, on_device(): limits = jnp.where(block_mask > 0, obs_valid[None], 0).astype(jnp.bfloat16)  0.69 us
  transfers between devices with their start and end apart: 4, of which 2 were waited for; matrix products, arithmetic and copies ran while one was open for 11% of the time, Pallas kernels for 15%

profile of v4, /device:TPU:0, one launch (start us, length us, event | category | flops | bytes accessed | tf_op | source)
XLA Modules:
  0.0 29.1 jit_solution(8582218819771746908)
XLA Ops:
  0.0 1.5 %broadcast_select_fusion.2 = bf16[16,2,8,512]{3,2,1,0:T(8,128)(2,1)} fusion(pred[2]{0:T(512)(128)(4,1)S(1)} %iota_compare_fusion, bf16[8,512]{1,0:T(8,128)(2,1)} %param.11, bf16[8,512]{1,0:T(8,128)(2,1)} %param.10), kind=kLoop, calls=%fused_computation.4 | loop fusion | flops 131072 | bytes 278530 | tf_op jit(solution)/shard_map/jit(_where)/select_n | solution.py:186
  1.5 8.3 %all-to-all-start = ((bf16[16,2,8,512]{3,2,1,0:T(8,128)(2,1)}), bf16[16,2,8,512]{3,2,1,0:T(8,128)(2,1)S(1)}, u32[]{:S(2)}, u32[]{:S(2)}) async-start(bf16[16,2,8,512]{3,2,1,0:T(8,128)(2,1)} %broadcast_select_fusion.2), calls=%async_computation | async-start | bytes 524288 | tf_op jit(solution)/shard_map/all_to_all | solution.py:187
  9.9 1.1 %fusion.2 = (bf16[128,512]{1,0:T(8,128)(2,1)S(1)}, bf16[128,512]{1,0:T(8,128)(2,1)S(1)}, bf16[128,512]{1,0:T(8,128)(2,1)S(1)}, bf16[128,512]{1,0:T(8,128)(2,1)S(1)}) fusion(bf16[256,512]{1,0:T(8,128)(2,1)} %param.8, bf16[256,512]{1,0:T(8,128)(2,1)} %param.9), kind=kLoop, calls=%fused_computation.12 | loop fusion | bytes 1048576 | tf_op jit(solution)/shard_map/split | solution.py:193
  11.0 0.7 %fusion = bf16[2,2]{1,0:T(2,128)(2,1)S(1)} fusion(s32[2,2]{1,0:T(2,128)} %param.12, s32[2]{0:T(128)} %param.13), kind=kLoop, calls=%fused_computation.8 | loop fusion | flops 12 | bytes 32 | tf_op jit(solution)/shard_map/convert_element_type | solution.py:195
  11.7 0.1 broadcast_select_fusion
  11.8 0.1 collective-permute-start.2
  11.9 0.7 %collective-permute-start = (bf16[272,512]{1,0:T(8,128)(2,1)S(1)}, bf16[272,512]{1,0:T(8,128)(2,1)S(1)}, u32[]{:S(2)}, u32[]{:S(2)}) collective-permute-start(bf16[272,512]{1,0:T(8,128)(2,1)S(1)} %get-tuple-element.30.far_sent_ref), channel_id=1, source_target_pairs={{1,2},{3,4},{5,6},{7,8},{9,10},{11,12},{13,14},{15,16},{17,18},{19... | collective-permute-start | bytes 835592 | tf_op jit(solution)/shard_map/ppermute | solution.py:205
  12.6 7.9 %all-to-all-done.same_ref = bf16[16,2,8,512]{3,2,1,0:T(8,128)(2,1)S(1)} async-done(((bf16[16,2,8,512]{3,2,1,0:T(8,128)(2,1)}), bf16[16,2,8,512]{3,2,1,0:T(8,128)(2,1)S(1)}, u32[]{:S(2)}, u32[]{:S(2)}) %all-to-all-start) | async-done | bytes 262176 | tf_op jit(solution)/shard_map/all_to_all | solution.py:187
  20.5 0.0 collective-permute-start.1
  20.5 0.1 pad_add_fusion.meta_ref
  20.6 1.1 %fusion.1 = (bf16[256,512]{1,0:T(8,128)(2,1)S(1)}, bf16[256,512]{1,0:T(8,128)(2,1)S(1)}) fusion(bf16[512,512]{1,0:T(8,128)(2,1)} %param.14), kind=kLoop, calls=%fused_computation.11 | loop fusion | bytes 1048576 | tf_op jit(solution)/shard_map/split | solution.py:209
  21.7 0.0 collective-permute-done.2.near_ref
  21.7 0.4 %collective-permute-done.1.other_ref = bf16[16,2,8,512]{3,2,1,0:T(8,128)(2,1)S(1)} collective-permute-done((bf16[16,2,8,512]{3,2,1,0:T(8,128)(2,1)S(1)}, bf16[16,2,8,512]{3,2,1,0:T(8,128)(2,1)S(1)}, u32[]{:S(2)}, u32[]{:S(2)}) %collective-permute-start.1) | collective-permute-done | bytes 262176 | tf_op jit(solution)/shard_map/ppermute | solution.py:207
  22.1 4.4 %inner.1 = (bf16[128,512]{1,0:T(8,128)(2,1)S(1)}, f32[256,512]{1,0:T(8,128)S(1)}, bf16[512,256]{1,0:T(8,128)(2,1)S(1)}, bf16[3,512,512]{2,1,0:T(8,128)(2,1)S(1)}) custom-call(s32[2]{0:T(128)S(1)} %pad_add_fusion.meta_ref, bf16[272,512]{1,0:T(8,128)(2,1)S(1)} %collective-permute-done.2.near_ref, bf16[272,512]{1,0:T(8,128)(2,1)S(1)} %get-tuple-element.29.near_sent_ref, ...), custom_call_target="tpu_custom_call" | custom-call | flops 1409286144 | bytes 4718592 | tf_op jit(solution)/shard_map/inner/pallas_call | solution.py:220
  26.4 0.0 collective-permute-done.far_ref
  26.5 2.6 %outer.1 = bf16[256,512]{1,0:T(8,128)(2,1)} custom-call(s32[2]{0:T(128)S(1)} %pad_add_fusion.meta_ref, bf16[272,512]{1,0:T(8,128)(2,1)S(1)} %collective-permute-done.far_ref, bf16[16,2,8,512]{3,2,1,0:T(8,128)(2,1)S(1)} %all-to-all-done.same_ref, bf16[16,2,8,512]{3,2,1,0:T(8,128)(2,1)S(1)} %collective-permute-done.1.other_ref, ...), custom_call_target="tpu_custom_call" | custom-call | flops 603979776 | bytes 2359296 | tf_op jit(solution)/shard_map/outer/pallas_call | solution.py:242
  (4 shorter events, 0.0 us)
Async XLA Ops:
  1.5 19.0 %all-to-all-start = ((bf16[16,2,8,512]{3,2,1,0:T(8,128)(2,1)}), bf16[16,2,8,512]{3,2,1,0:T(8,128)(2,1)S(1)}, u32[]{:S(2)}, u32[]{:S(2)}) async-start(bf16[16,2,8,512]{3,2,1,0:T(8,128)(2,1)} %broadcast_select_fusion.2), calls=%async_computation | async-start | bytes 524288 | tf_op jit(solution)/shard_map/all_to_all | solution.py:187
  11.8 9.8 %collective-permute-start.2 = (bf16[272,512]{1,0:T(8,128)(2,1)S(1)}, bf16[272,512]{1,0:T(8,128)(2,1)S(1)}, u32[]{:S(2)}, u32[]{:S(2)}) collective-permute-start(bf16[272,512]{1,0:T(8,128)(2,1)S(1)} %get-tuple-element.29.near_sent_ref), channel_id=1, source_target_pairs={{0,1},{1,0},{2,3},{3,2},{4,5},{5,4},{6,7},{7,6},{8,9},{9,8},{10,11... | collective-permute-start | bytes 835592 | tf_op jit(solution)/shard_map/ppermute | solution.py:206
  11.9 14.5 %collective-permute-start = (bf16[272,512]{1,0:T(8,128)(2,1)S(1)}, bf16[272,512]{1,0:T(8,128)(2,1)S(1)}, u32[]{:S(2)}, u32[]{:S(2)}) collective-permute-start(bf16[272,512]{1,0:T(8,128)(2,1)S(1)} %get-tuple-element.30.far_sent_ref), channel_id=1, source_target_pairs={{1,2},{3,4},{5,6},{7,8},{9,10},{11,12},{13,14},{15,16},{17,18},{19... | collective-permute-start | bytes 835592 | tf_op jit(solution)/shard_map/ppermute | solution.py:205
  20.5 1.5 %collective-permute-start.1 = (bf16[16,2,8,512]{3,2,1,0:T(8,128)(2,1)S(1)}, bf16[16,2,8,512]{3,2,1,0:T(8,128)(2,1)S(1)}, u32[]{:S(2)}, u32[]{:S(2)}) collective-permute-start(bf16[16,2,8,512]{3,2,1,0:T(8,128)(2,1)S(1)} %all-to-all-done.same_ref), channel_id=1, source_target_pairs={{0,1},{1,0},{2,3},{3,2},{4,5},{5,4},{6,7},{7,6},{8,9},{9,8},{10,11... | collective-permute-start | bytes 786440 | tf_op jit(solution)/shard_map/ppermute | solution.py:207

commit v5 on v4

--- a/solution.py
+++ b/solution.py
@@ -117,7 +117,7 @@
         for lon_off in range(3)
         for i, source in enumerate((1, 2 - 2 * core))
     ]
-    copies.append(pltpu.make_async_copy(conv_hbm.at[2 * core], last_ref, sems.at[6]))
+    copies.append(pltpu.make_async_copy(conv_hbm.at[2 * core, :2], last_ref, sems.at[6]))
     for copy in copies:
         copy.start()
 
@@ -149,9 +149,11 @@
 def outer_kernel(
     lon, width, nblocks, rows,
     meta_ref, far_ref, same_ref, other_ref, upper_ref, lower_ref, edge_ref, partial_ref, keys_ref,
-    conv_ref, out_ref, mixed_ref,
+    taps_ref, conv_hbm, out_ref, conv_ref, mixed_ref, sem,
 ):
     core = meta_ref[0]
+    copy = pltpu.make_async_copy(conv_hbm.at[2 * core, 2], conv_ref, sem)
+    copy.start()
     _, normed = attend(
         lon, width, nblocks, rows, core, (far_ref,), lambda cols: keys_ref[cols, :],
         same_ref, other_ref, (upper_ref, lower_ref), mixed_ref,
@@ -159,8 +161,10 @@
     far = jnp.where(meta_ref[1] > 0, normed, 0.0).astype(jnp.bfloat16)
     field = jnp.concatenate([edge_ref[...], far], axis=0)
     terms = [
-        jnp.dot(field, conv_ref[lon_off], preferred_element_type=jnp.float32) for lon_off in range(3)
+        jnp.dot(field, taps_ref[lon_off], preferred_element_type=jnp.float32) for lon_off in range(2)
     ]
+    copy.wait()
+    terms.append(jnp.dot(field, conv_ref[...], preferred_element_type=jnp.float32))
     for start, tile in ((0, 1 - core), (lon, core)):
         here = slice(start, start + lon)
         total = partial_ref[here, :] + around([term[here] for term in terms], lon)
@@ -180,11 +184,11 @@
     me = lax.axis_index(AXES)
     core = me % CORES
 
+    block = jnp.stack([obs_keys, obs_values])
     groups = [list(range(c, devices, CORES)) for c in range(CORES)]
-    shape = (pairs, 2) + obs_keys.shape
-    is_key = lax.broadcasted_iota(jnp.int32, shape, 1) == 0
-    blocks = jnp.where(is_key, obs_keys[None, None], obs_values[None, None])
-    same = lax.all_to_all(blocks, AXES, 0, 0, axis_index_groups=groups)
+    same = lax.all_to_all(
+        jnp.broadcast_to(block[None], (pairs,) + block.shape), AXES, 0, 0, axis_index_groups=groups
+    )
     swap = [(i, i ^ 1) for i in range(devices)]
     across = [(i, i + 1) for i in range(1, devices - 1, CORES)]
     across += [(target, source) for source, target in across]
@@ -202,8 +206,8 @@
     first, last = packed(0), packed(tiles - 1)
     far_sent = jnp.where(core == 0, first, last)
     near_sent = jnp.where(core == 0, last, first)
+    near = lax.ppermute(near_sent, AXES, swap)
     far = lax.ppermute(far_sent, AXES, across)
-    near = lax.ppermute(near_sent, AXES, swap)
     other = lax.ppermute(same, AXES, swap)
     out_weight, _ = lax.optimization_barrier((out_weight, same))
     upper, lower = lax.optimization_barrier(tuple(jnp.split(out_weight, 2, axis=0)))
@@ -223,7 +227,7 @@
             jax.ShapeDtypeStruct((lon, width), jnp.bfloat16),
             jax.ShapeDtypeStruct((q_dev, width), jnp.float32),
             jax.ShapeDtypeStruct((width, obs), jnp.bfloat16),
-            jax.ShapeDtypeStruct(conv_weight.shape[1:], jnp.bfloat16),
+            jax.ShapeDtypeStruct((2, width, width), jnp.bfloat16),
         ],
         in_specs=[smem] + [vmem] * 7 + [hbm],
         out_specs=[vmem] * 4,
@@ -242,17 +246,19 @@
     return pl.pallas_call(
         functools.partial(outer_kernel, *sizes),
         out_shape=jax.ShapeDtypeStruct((q_dev, width), jnp.bfloat16),
-        in_specs=[smem] + [vmem] * 9,
+        in_specs=[smem] + [vmem] * 9 + [hbm],
         out_specs=vmem,
         scratch_shapes=[
+            pltpu.VMEM((width, width), jnp.bfloat16),
             pltpu.VMEM((lon, width), jnp.bfloat16),
+            pltpu.SemaphoreType.DMA,
         ],
         compiler_params=params,
         cost_estimate=pl.CostEstimate(
             flops=row_flops + 6 * tap_flops, bytes_accessed=conv_weight.size, transcendentals=0
         ),
         name="outer",
-    )(meta, far, same, other, upper, lower, edge, partial, keys, taps)
+    )(meta, far, same, other, upper, lower, edge, partial, keys, taps, conv_weight)
 
 
 def solution(mesh):

time: 29.5 us -> 30.4 us (1.031)
  Pallas kernels: 7.01 us -> 8.01 us
  other arithmetic: 2.38 us -> 1.58 us
  local copies, waits for them, and re-layouts: 2.24 us -> 2.97 us
    select_n x1 -> x0, other arithmetic: 1.51 us -> none  [on_device(): blocks = jnp.where(is_key, obs_keys[None, None], obs_values[None, None])]
    pallas_call x1, Pallas kernels: 2.63 us -> 3.64 us  [on_device(): pl.pallas_call(functools.partial(outer_kernel, *sizes), out_shape=jax.Sha...]
    broadcast_in_dim x0 -> x1, local copies, waits for them, and re-layouts: none -> 0.73 us  [on_device(): jnp.broadcast_to(block[None], (pairs,) + block.shape)]
    another operation x0 -> x1, other arithmetic: none -> 0.72 us  [on_device(): block = jnp.stack([obs_keys, obs_values])]
  transfers between devices with their start and end apart: 4 -> 4, of which waited for: 2 -> 2; matrix products, arithmetic and copies ran while one was open for 11% -> 10% of each run, Pallas kernels for 15% -> 15%
where the time goes in v5:
time: 30.4 us; the launch traced here: 30 us
  starting transfers between devices  9.06 us (30%)
  waiting for transfers between devices  8.3 us (27%)
  Pallas kernels  8.01 us (26%)
  local copies, waits for them, and re-layouts  2.97 us (10%)
  other arithmetic  1.58 us (5%)
    all_to_all x1, starting transfers between devices, on_device(): lax.all_to_all(jnp.broadcast_to(block[None], (pairs,) + block.shape), AXE...  8.31 us
    all_to_all x1, waiting for transfers between devices, on_device(): lax.all_to_all(jnp.broadcast_to(block[None], (pairs,) + block.shape), AXE...  7.91 us
    pallas_call x1, Pallas kernels, on_device(): pl.pallas_call(functools.partial(inner_kernel, *sizes), out_shape=[jax.Sh...  4.38 us
    pallas_call x1, Pallas kernels, on_device(): pl.pallas_call(functools.partial(outer_kernel, *sizes), out_shape=jax.Sha...  3.64 us
    split x1, local copies, waits for them, and re-layouts, on_device(): jnp.split(grid_feat, tiles, axis=0)  1.13 us
    split x1, local copies, waits for them, and re-layouts, on_device(): jnp.split(out_weight, 2, axis=0)  1.06 us
    broadcast_in_dim x1, local copies, waits for them, and re-layouts, on_device(): jnp.broadcast_to(block[None], (pairs,) + block.shape)  0.73 us
    another operation x1, other arithmetic, on_device(): block = jnp.stack([obs_keys, obs_values])  0.72 us
  transfers between devices with their start and end apart: 4, of which 2 were waited for; matrix products, arithmetic and copies ran while one was open for 10% of the time, Pallas kernels for 15%

profile of v5, /device:TPU:0, one launch (start us, length us, event | category | flops | bytes accessed | tf_op | source)
XLA Modules:
  0.0 30.0 jit_solution(8748226071413615939)
XLA Ops:
  0.0 0.7 %pad_maximum_fusion.2 = bf16[2,8,512]{2,1,0:T(8,128)(2,1)S(1)} fusion(bf16[1,8,512]{2,1,0:T(8,128)(2,1)} %bitcast.4, bf16[1,8,512]{2,1,0:T(8,128)(2,1)} %bitcast.5), kind=kLoop, calls=%fused_computation.4 | loop fusion | flops 8192 | bytes 32768 | tf_op jit(solution)/shard_map/stack | solution.py:187
  0.7 0.7 %broadcast_in_dim.36 = bf16[16,2,8,512]{3,2,1,0:T(8,128)(2,1)} broadcast(bf16[2,8,512]{2,1,0:T(8,128)(2,1)S(1)} %pad_maximum_fusion.2), dimensions={1,2,3} | broadcast | bytes 278528 | tf_op jit(solution)/shard_map/broadcast_in_dim | solution.py:190
  1.5 8.3 %all-to-all-start = ((bf16[16,2,8,512]{3,2,1,0:T(8,128)(2,1)}), bf16[16,2,8,512]{3,2,1,0:T(8,128)(2,1)S(1)}, u32[]{:S(2)}, u32[]{:S(2)}) async-start(bf16[16,2,8,512]{3,2,1,0:T(8,128)(2,1)} %broadcast_in_dim.36), calls=%async_computation | async-start | bytes 524288 | tf_op jit(solution)/shard_map/all_to_all | solution.py:189
  9.8 1.1 %fusion.2 = (bf16[128,512]{1,0:T(8,128)(2,1)S(1)}, bf16[128,512]{1,0:T(8,128)(2,1)S(1)}, bf16[128,512]{1,0:T(8,128)(2,1)S(1)}, bf16[128,512]{1,0:T(8,128)(2,1)S(1)}) fusion(bf16[256,512]{1,0:T(8,128)(2,1)} %param.8, bf16[256,512]{1,0:T(8,128)(2,1)} %param.9), kind=kLoop, calls=%fused_computation.11 | loop fusion | bytes 1048576 | tf_op jit(solution)/shard_map/split | solution.py:197
  10.9 0.7 %fusion = bf16[2,2]{1,0:T(2,128)(2,1)S(1)} fusion(s32[2,2]{1,0:T(2,128)} %param.12, s32[2]{0:T(128)} %param.13), kind=kLoop, calls=%fused_computation.8 | loop fusion | flops 12 | bytes 32 | tf_op jit(solution)/shard_map/convert_element_type | solution.py:199
  11.7 0.1 broadcast_select_fusion
  11.8 0.1 collective-permute-start.2
  11.8 0.7 %collective-permute-start = (bf16[272,512]{1,0:T(8,128)(2,1)S(1)}, bf16[272,512]{1,0:T(8,128)(2,1)S(1)}, u32[]{:S(2)}, u32[]{:S(2)}) collective-permute-start(bf16[272,512]{1,0:T(8,128)(2,1)S(1)} %get-tuple-element.30.far_sent_ref), channel_id=1, source_target_pairs={{1,2},{3,4},{5,6},{7,8},{9,10},{11,12},{13,14},{15,16},{17,18},{19... | collective-permute-start | bytes 835592 | tf_op jit(solution)/shard_map/ppermute | solution.py:210
  12.5 7.9 %all-to-all-done.same_ref = bf16[16,2,8,512]{3,2,1,0:T(8,128)(2,1)S(1)} async-done(((bf16[16,2,8,512]{3,2,1,0:T(8,128)(2,1)}), bf16[16,2,8,512]{3,2,1,0:T(8,128)(2,1)S(1)}, u32[]{:S(2)}, u32[]{:S(2)}) %all-to-all-start) | async-done | bytes 262176 | tf_op jit(solution)/shard_map/all_to_all | solution.py:189
  20.5 0.0 collective-permute-start.1
  20.5 0.1 pad_add_fusion.meta_ref
  20.5 1.1 %fusion.1 = (bf16[256,512]{1,0:T(8,128)(2,1)S(1)}, bf16[256,512]{1,0:T(8,128)(2,1)S(1)}) fusion(bf16[512,512]{1,0:T(8,128)(2,1)} %param.14), kind=kLoop, calls=%fused_computation.10 | loop fusion | bytes 1048576 | tf_op jit(solution)/shard_map/split | solution.py:213
  21.6 0.0 collective-permute-done.2.near_ref
  21.6 0.4 %collective-permute-done.1.other_ref = bf16[16,2,8,512]{3,2,1,0:T(8,128)(2,1)S(1)} collective-permute-done((bf16[16,2,8,512]{3,2,1,0:T(8,128)(2,1)S(1)}, bf16[16,2,8,512]{3,2,1,0:T(8,128)(2,1)S(1)}, u32[]{:S(2)}, u32[]{:S(2)}) %collective-permute-start.1) | collective-permute-done | bytes 262176 | tf_op jit(solution)/shard_map/ppermute | solution.py:211
  22.0 4.4 %inner.1 = (bf16[128,512]{1,0:T(8,128)(2,1)S(1)}, f32[256,512]{1,0:T(8,128)S(1)}, bf16[512,256]{1,0:T(8,128)(2,1)S(1)}, bf16[2,512,512]{2,1,0:T(8,128)(2,1)S(1)}) custom-call(s32[2]{0:T(128)S(1)} %pad_add_fusion.meta_ref, bf16[272,512]{1,0:T(8,128)(2,1)S(1)} %collective-permute-done.2.near_ref, bf16[272,512]{1,0:T(8,128)(2,1)S(1)} %get-tuple-element.29.near_sent_ref, ...), custom_call_target="tpu_custom_call" | custom-call | flops 1409286144 | bytes 4718592 | tf_op jit(solution)/shard_map/inner/pallas_call | solution.py:224
  26.4 0.0 collective-permute-done.far_ref
  26.4 3.6 %outer.1 = bf16[256,512]{1,0:T(8,128)(2,1)} custom-call(s32[2]{0:T(128)S(1)} %pad_add_fusion.meta_ref, bf16[272,512]{1,0:T(8,128)(2,1)S(1)} %collective-permute-done.far_ref, bf16[16,2,8,512]{3,2,1,0:T(8,128)(2,1)S(1)} %all-to-all-done.same_ref, bf16[16,2,8,512]{3,2,1,0:T(8,128)(2,1)S(1)} %collective-permute-done.1.other_ref, ...), custom_call_target="tpu_custom_call" | custom-call | flops 603979776 | bytes 2359296 | tf_op jit(solution)/shard_map/outer/pallas_call | solution.py:246
  (3 shorter events, 0.0 us)
Async XLA Ops:
  1.5 19.0 %all-to-all-start = ((bf16[16,2,8,512]{3,2,1,0:T(8,128)(2,1)}), bf16[16,2,8,512]{3,2,1,0:T(8,128)(2,1)S(1)}, u32[]{:S(2)}, u32[]{:S(2)}) async-start(bf16[16,2,8,512]{3,2,1,0:T(8,128)(2,1)} %broadcast_in_dim.36), calls=%async_computation | async-start | bytes 524288 | tf_op jit(solution)/shard_map/all_to_all | solution.py:189
  11.8 9.8 %collective-permute-start.2 = (bf16[272,512]{1,0:T(8,128)(2,1)S(1)}, bf16[272,512]{1,0:T(8,128)(2,1)S(1)}, u32[]{:S(2)}, u32[]{:S(2)}) collective-permute-start(bf16[272,512]{1,0:T(8,128)(2,1)S(1)} %get-tuple-element.29.near_sent_ref), channel_id=1, source_target_pairs={{0,1},{1,0},{2,3},{3,2},{4,5},{5,4},{6,7},{7,6},{8,9},{9,8},{10,11... | collective-permute-start | bytes 835592 | tf_op jit(solution)/shard_map/ppermute | solution.py:209
  11.8 14.5 %collective-permute-start = (bf16[272,512]{1,0:T(8,128)(2,1)S(1)}, bf16[272,512]{1,0:T(8,128)(2,1)S(1)}, u32[]{:S(2)}, u32[]{:S(2)}) collective-permute-start(bf16[272,512]{1,0:T(8,128)(2,1)S(1)} %get-tuple-element.30.far_sent_ref), channel_id=1, source_target_pairs={{1,2},{3,4},{5,6},{7,8},{9,10},{11,12},{13,14},{15,16},{17,18},{19... | collective-permute-start | bytes 835592 | tf_op jit(solution)/shard_map/ppermute | solution.py:210
  20.5 1.5 %collective-permute-start.1 = (bf16[16,2,8,512]{3,2,1,0:T(8,128)(2,1)S(1)}, bf16[16,2,8,512]{3,2,1,0:T(8,128)(2,1)S(1)}, u32[]{:S(2)}, u32[]{:S(2)}) collective-permute-start(bf16[16,2,8,512]{3,2,1,0:T(8,128)(2,1)S(1)} %all-to-all-done.same_ref), channel_id=1, source_target_pairs={{0,1},{1,0},{2,3},{3,2},{4,5},{5,4},{6,7},{7,6},{8,9},{9,8},{10,11... | collective-permute-start | bytes 786440 | tf_op jit(solution)/shard_map/ppermute | solution.py:211

commit v6 on v4

--- a/solution.py
+++ b/solution.py
@@ -107,19 +107,9 @@
 def inner_kernel(
     lon, width, nblocks, rows,
     meta_ref, near_ref, near_sent_ref, far_sent_ref, same_ref, other_ref, upper_ref, lower_ref,
-    conv_hbm, edge_ref, partial_ref, keys_ref, last_ref, conv_ref, mixed_ref, field_ref, sems,
+    conv_ref, edge_ref, partial_ref, keys_ref, mixed_ref, field_ref,
 ):
     core = meta_ref[0]
-    copies = [
-        pltpu.make_async_copy(
-            conv_hbm.at[source, lon_off], conv_ref.at[i, lon_off], sems.at[2 * lon_off + i]
-        )
-        for lon_off in range(3)
-        for i, source in enumerate((1, 2 - 2 * core))
-    ]
-    copies.append(pltpu.make_async_copy(conv_hbm.at[2 * core], last_ref, sems.at[6]))
-    for copy in copies:
-        copy.start()
 
     def keys_of(cols):
         keys = both_cores(same_ref, other_ref, 0, cols).T
@@ -135,15 +125,12 @@
     inputs = jnp.concatenate([field_ref[lon:, :], field_ref[: 2 * lon, :]], axis=1)
     terms = []
     for lon_off in range(3):
-        for copy in copies[2 * lon_off : 2 * lon_off + 2]:
-            copy.wait()
-        taps = conv_ref[:, lon_off].reshape(2 * width, width)
+        taps = jnp.concatenate([conv_ref[1, lon_off], conv_ref[2 - 2 * core, lon_off]], axis=0)
         terms.append(jnp.dot(inputs, taps, preferred_element_type=jnp.float32))
     for start in (0, lon):
         here = slice(start, start + lon)
         shifted = around([term[here] for term in terms], lon)
         partial_ref[here, :] = wide[start + lon : start + 2 * lon] + shifted
-    copies[6].wait()
 
 
 def outer_kernel(
@@ -159,12 +146,27 @@
     far = jnp.where(meta_ref[1] > 0, normed, 0.0).astype(jnp.bfloat16)
     field = jnp.concatenate([edge_ref[...], far], axis=0)
     terms = [
-        jnp.dot(field, conv_ref[lon_off], preferred_element_type=jnp.float32) for lon_off in range(3)
+        jnp.dot(field, conv_ref[2 * core, lon_off], preferred_element_type=jnp.float32)
+        for lon_off in range(3)
     ]
     for start, tile in ((0, 1 - core), (lon, core)):
         here = slice(start, start + lon)
         total = partial_ref[here, :] + around([term[here] for term in terms], lon)
         out_ref[pl.ds(pl.multiple_of(tile * lon, lon), lon), :] = total.astype(jnp.bfloat16)
+
+
+def pack_kernel(lon, *refs):
+    queries_refs, grid_refs, limit_refs = refs[:2], refs[2:4], refs[4:6]
+    near_ref, far_ref = refs[6:]
+    even = lax.axis_index("tile") % CORES == 0
+    for place, pair_refs in (
+        (slice(0, lon), queries_refs),
+        (slice(lon, 2 * lon), grid_refs),
+        (slice(2 * lon, 2 * lon + LIMIT_ROWS), limit_refs),
+    ):
+        first, last = pair_refs[0][...], pair_refs[1][...]
+        far_ref[place, :] = jnp.where(even, first, last)
+        near_ref[place, :] = jnp.where(even, last, first)
 
 
 def on_device(
@@ -180,11 +182,11 @@
     me = lax.axis_index(AXES)
     core = me % CORES
 
+    block = jnp.stack([obs_keys, obs_values])
     groups = [list(range(c, devices, CORES)) for c in range(CORES)]
-    shape = (pairs, 2) + obs_keys.shape
-    is_key = lax.broadcasted_iota(jnp.int32, shape, 1) == 0
-    blocks = jnp.where(is_key, obs_keys[None, None], obs_values[None, None])
-    same = lax.all_to_all(blocks, AXES, 0, 0, axis_index_groups=groups)
+    same = lax.all_to_all(
+        jnp.broadcast_to(block[None], (pairs,) + block.shape), AXES, 0, 0, axis_index_groups=groups
+    )
     swap = [(i, i ^ 1) for i in range(devices)]
     across = [(i, i + 1) for i in range(1, devices - 1, CORES)]
     across += [(target, source) for source, target in across]
@@ -195,13 +197,19 @@
     limits = jnp.where(block_mask > 0, obs_valid[None], 0).astype(jnp.bfloat16)
     limits = jnp.pad(limits, ((0, 0), (0, width - nblocks)))
 
-    def packed(tile):
-        limit = jnp.broadcast_to(limits[tile][None], (LIMIT_ROWS, width))
-        return jnp.concatenate([query_rows[tile], grid_rows[tile], limit], axis=0)
-
-    first, last = packed(0), packed(tiles - 1)
-    far_sent = jnp.where(core == 0, first, last)
-    near_sent = jnp.where(core == 0, last, first)
+    limit_rows = [
+        jnp.broadcast_to(limits[tile][None], (LIMIT_ROWS, width)) for tile in range(tiles)
+    ]
+    vmem = pl.BlockSpec(memory_space=pltpu.VMEM)
+    payload = jax.ShapeDtypeStruct((2 * lon + LIMIT_ROWS, width), jnp.bfloat16)
+    near_sent, far_sent = pl.pallas_call(
+        functools.partial(pack_kernel, lon),
+        out_shape=[payload] * 2,
+        in_specs=[vmem] * 6,
+        out_specs=[vmem] * 2,
+        cost_estimate=pl.CostEstimate(flops=10**10, bytes_accessed=4 * payload.size * 2, transcendentals=0),
+        name="pack",
+    )(*query_rows, *grid_rows, *limit_rows)
     far = lax.ppermute(far_sent, AXES, across)
     near = lax.ppermute(near_sent, AXES, swap)
     other = lax.ppermute(same, AXES, swap)
@@ -211,27 +219,22 @@
     far_exists = (me > 0) & (me < devices - 1)
     meta = jnp.stack([core, far_exists.astype(core.dtype)]).astype(jnp.int32)
 
-    vmem = pl.BlockSpec(memory_space=pltpu.VMEM)
     smem = pl.BlockSpec(memory_space=pltpu.SMEM)
-    hbm = pl.BlockSpec(memory_space=pltpu.HBM)
     sizes = (lon, width, nblocks, rows)
-    params = pltpu.CompilerParams(vmem_limit_bytes=48 * 2**20)
+    params = pltpu.CompilerParams(vmem_limit_bytes=40 * 2**20)
     tap_flops, row_flops = 2 * lon * width * width, 2 * lon * width * (width + 4 * obs)
-    edge, partial, keys, taps = pl.pallas_call(
+    edge, partial, keys = pl.pallas_call(
         functools.partial(inner_kernel, *sizes),
         out_shape=[
             jax.ShapeDtypeStruct((lon, width), jnp.bfloat16),
             jax.ShapeDtypeStruct((q_dev, width), jnp.float32),
             jax.ShapeDtypeStruct((width, obs), jnp.bfloat16),
-            jax.ShapeDtypeStruct(conv_weight.shape[1:], jnp.bfloat16),
         ],
-        in_specs=[smem] + [vmem] * 7 + [hbm],
-        out_specs=[vmem] * 4,
+        in_specs=[smem] + [vmem] * 8,
+        out_specs=[vmem] * 3,
         scratch_shapes=[
-            pltpu.VMEM((2,) + conv_weight.shape[1:], jnp.bfloat16),
             pltpu.VMEM((3 * lon, width), jnp.bfloat16),
             pltpu.VMEM((3 * lon, width), jnp.bfloat16),
-            pltpu.SemaphoreType.DMA((7,)),
         ],
         compiler_params=params,
         cost_estimate=pl.CostEstimate(
@@ -252,7 +255,7 @@
             flops=row_flops + 6 * tap_flops, bytes_accessed=conv_weight.size, transcendentals=0
         ),
         name="outer",
-    )(meta, far, same, other, upper, lower, edge, partial, keys, taps)
+    )(meta, far, same, other, upper, lower, edge, partial, keys, conv_weight)
 
 
 def solution(mesh):

time: 29.5 us -> 35.6 us (1.21)
  the two profiles are of different devices: /device:TPU:0 before, /device:TPU:5 now
where the time goes in v6:
time: 35.6 us; the launch traced here: 35.1 us
  starting transfers between devices  14.2 us (40%)
  local copies, waits for them, and re-layouts  10.5 us (29%)
  Pallas kernels  7.87 us (22%)
  other arithmetic  1.48 us (4%)
  waiting for transfers between devices  1.04 us (3%)
    all_to_all x1, starting transfers between devices, on_device(): lax.all_to_all(jnp.broadcast_to(block[None], (pairs,) + block.shape), AXE...  6.72 us
    unnamed x10, local copies, waits for them, and re-layouts  6.58 us
    ppermute x1, starting transfers between devices, on_device(): other = lax.ppermute(same, AXES, swap)  3.27 us
    pallas_call x1, Pallas kernels, on_device(): pl.pallas_call(functools.partial(inner_kernel, *sizes), out_shape=[jax.Sh...  3.23 us
    ppermute x1, starting transfers between devices, on_device(): far = lax.ppermute(far_sent, AXES, across)  2.97 us
    pallas_call x1, Pallas kernels, on_device(): pl.pallas_call(functools.partial(outer_kernel, *sizes), out_shape=jax.Sha...  2.63 us
    pallas_call x1, Pallas kernels, on_device(): pl.pallas_call(functools.partial(pack_kernel, lon), out_shape=[payload] *...  2.01 us
    split x1, local copies, waits for them, and re-layouts, on_device(): jnp.split(grid_feat, tiles, axis=0)  1.89 us
  transfers between devices with their start and end apart: 4, of which 1 were waited for; matrix products, arithmetic and copies ran while one was open for 11% of the time, Pallas kernels for 15%

profile of v6, /device:TPU:5, one launch (start us, length us, event | category | flops | bytes accessed | tf_op | source)
XLA Modules:
  0.0 35.1 jit_solution(6615141417302522502)
XLA Ops:
  0.0 0.7 %pad_maximum_fusion = bf16[2,8,512]{2,1,0:T(8,128)(2,1)S(1)} fusion(bf16[1,8,512]{2,1,0:T(8,128)(2,1)} %bitcast.4, bf16[1,8,512]{2,1,0:T(8,128)(2,1)} %bitcast.5), kind=kLoop, calls=%fused_computation | loop fusion | flops 8192 | bytes 32768 | tf_op jit(solution)/shard_map/stack | solution.py:185
  0.7 0.7 %broadcast_in_dim.36 = bf16[16,2,8,512]{3,2,1,0:T(8,128)(2,1)} broadcast(bf16[2,8,512]{2,1,0:T(8,128)(2,1)S(1)} %pad_maximum_fusion), dimensions={1,2,3} | broadcast | bytes 278528 | tf_op jit(solution)/shard_map/broadcast_in_dim | solution.py:188
  1.5 6.7 %all-to-all-start = ((bf16[16,2,8,512]{3,2,1,0:T(8,128)(2,1)}), bf16[16,2,8,512]{3,2,1,0:T(8,128)(2,1)S(1)}, u32[]{:S(2)}, u32[]{:S(2)}) async-start(bf16[16,2,8,512]{3,2,1,0:T(8,128)(2,1)} %broadcast_in_dim.36), calls=%async_computation | async-start | bytes 524288 | tf_op jit(solution)/shard_map/all_to_all | solution.py:187
  8.2 1.9 %fusion.2 = (bf16[128,512]{1,0:T(8,128)(2,1)}, bf16[128,512]{1,0:T(8,128)(2,1)}, bf16[128,512]{1,0:T(8,128)(2,1)}, bf16[128,512]{1,0:T(8,128)(2,1)}) fusion(bf16[256,512]{1,0:T(8,128)(2,1)} %param.8, bf16[256,512]{1,0:T(8,128)(2,1)} %param.9), kind=kLoop, calls=%fused_computation.7 | loop fusion | bytes 1048576 | tf_op jit(solution)/shard_map/split | solution.py:195
  10.1 0.7 %fusion = bf16[2,2]{1,0:T(2,128)(2,1)S(1)} fusion(s32[2,2]{1,0:T(2,128)} %param.12, s32[2]{0:T(128)} %param.13), kind=kLoop, calls=%fused_computation.4 | loop fusion | flops 12 | bytes 32 | tf_op jit(solution)/shard_map/convert_element_type | solution.py:197
  10.8 0.6 %broadcast_in_dim.33.refs_4_ = bf16[16,512]{1,0:T(8,128)(2,1)} broadcast(bf16[512]{0:T(512)(128)(2,1)S(1)} %get-tuple-element.30), dimensions={1} | broadcast | bytes 17408 | tf_op jit(solution)/shard_map/broadcast_in_dim | solution.py:201
  11.4 0.6 %broadcast_in_dim.35.refs_5_ = bf16[16,512]{1,0:T(8,128)(2,1)} broadcast(bf16[512]{0:T(512)(128)(2,1)S(1)} %get-tuple-element.29), dimensions={1} | broadcast | bytes 17408 | tf_op jit(solution)/shard_map/broadcast_in_dim | solution.py:201
  12.0 2.0 %pack.1 = (bf16[272,512]{1,0:T(8,128)(2,1)}, bf16[272,512]{1,0:T(8,128)(2,1)}) custom-call(bf16[128,512]{1,0:T(8,128)(2,1)} %get-tuple-element.17.refs_0_, bf16[128,512]{1,0:T(8,128)(2,1)} %get-tuple-element.18.refs_1_, bf16[128,512]{1,0:T(8,128)(2,1)} %get-tuple-element.19.refs_2_, bf16[128,512]{1,0:T(8,128)(2,1)} %get-tuple-element.20.refs_3_, ...), custom_call_target="tpu_custom_call" | custom-call | flops 10000000000 | bytes 1114112 | tf_op jit(solution)/shard_map/pack/pallas_call | solution.py:205
  14.0 1.2 %collective-permute-start.2 = (bf16[272,512]{1,0:T(8,128)(2,1)}, bf16[272,512]{1,0:T(8,128)(2,1)S(1)}, u32[]{:S(2)}, u32[]{:S(2)}) collective-permute-start(bf16[272,512]{1,0:T(8,128)(2,1)} %get-tuple-element.25.near_sent_ref), channel_id=1, source_target_pairs={{0,1},{1,0},{2,3},{3,2},{4,5},{5,4},{6,7},{7,6},{8,9},{9,8},{10,11... | collective-permute-start | bytes 835592 | tf_op jit(solution)/shard_map/ppermute | solution.py:214
  15.2 3.0 %collective-permute-start = (bf16[272,512]{1,0:T(8,128)(2,1)}, bf16[272,512]{1,0:T(8,128)(2,1)S(1)}, u32[]{:S(2)}, u32[]{:S(2)}) collective-permute-start(bf16[272,512]{1,0:T(8,128)(2,1)} %get-tuple-element.21.far_sent_ref), channel_id=1, source_target_pairs={{1,2},{3,4},{5,6},{7,8},{9,10},{11,12},{13,14},{15,16},{17,18},{19... | collective-permute-start | bytes 835592 | tf_op jit(solution)/shard_map/ppermute | solution.py:213
  18.2 0.0 all-to-all-done.same_ref
  18.2 3.3 %collective-permute-start.1 = (bf16[16,2,8,512]{3,2,1,0:T(8,128)(2,1)S(1)}, bf16[16,2,8,512]{3,2,1,0:T(8,128)(2,1)S(1)}, u32[]{:S(2)}, u32[]{:S(2)}) collective-permute-start(bf16[16,2,8,512]{3,2,1,0:T(8,128)(2,1)S(1)} %all-to-all-done.same_ref), channel_id=1, source_target_pairs={{0,1},{1,0},{2,3},{3,2},{4,5},{5,4},{6,7},{7,6},{8,9},{9,8},{10,11... | collective-permute-start | bytes 786440 | tf_op jit(solution)/shard_map/ppermute | solution.py:215
  21.5 0.1 pad_add_fusion.meta_ref
  21.6 0.0 copy-done.4
  21.6 0.0 collective-permute-done.2.near_ref
  21.6 1.0 %collective-permute-done.1.other_ref = bf16[16,2,8,512]{3,2,1,0:T(8,128)(2,1)S(1)} collective-permute-done((bf16[16,2,8,512]{3,2,1,0:T(8,128)(2,1)S(1)}, bf16[16,2,8,512]{3,2,1,0:T(8,128)(2,1)S(1)}, u32[]{:S(2)}, u32[]{:S(2)}) %collective-permute-start.1) | collective-permute-done | bytes 262176 | tf_op jit(solution)/shard_map/ppermute | solution.py:215
  22.7 2.3 %copy-done = bf16[3,3,512,512]{3,2,1,0:T(8,128)(2,1)S(1)} copy-done((bf16[3,3,512,512]{3,2,1,0:T(8,128)(2,1)S(1)}, bf16[3,3,512,512]{3,2,1,0:T(8,128)(2,1)}, u32[]{:S(2)}) %copy-start) | copy-done | bytes 4718616
  25.0 1.0 %copy-done.2 = bf16[272,512]{1,0:T(8,128)(2,1)S(1)} copy-done((bf16[272,512]{1,0:T(8,128)(2,1)S(1)}, bf16[272,512]{1,0:T(8,128)(2,1)}, u32[]{:S(2)}) %copy-start.2) | copy-done | bytes 278552
  26.0 1.0 %copy-done.3 = bf16[272,512]{1,0:T(8,128)(2,1)S(1)} copy-done((bf16[272,512]{1,0:T(8,128)(2,1)S(1)}, bf16[272,512]{1,0:T(8,128)(2,1)}, u32[]{:S(2)}) %copy-start.3) | copy-done | bytes 278552
  26.9 3.2 %inner.1 = (bf16[128,512]{1,0:T(8,128)(2,1)S(1)}, f32[256,512]{1,0:T(8,128)S(1)}, bf16[512,256]{1,0:T(8,128)(2,1)S(1)}) custom-call(s32[2]{0:T(128)S(1)} %pad_add_fusion.meta_ref, bf16[272,512]{1,0:T(8,128)(2,1)S(1)} %collective-permute-done.2.near_ref, bf16[272,512]{1,0:T(8,128)(2,1)S(1)} %copy-done.3, bf16[272,512]{1,0:T(8,128)(2,1)S(1)} %copy-done.2, ...), custom_call_target="tpu_custom_call" | custom-call | flops 1409286144 | bytes 4718592 | tf_op jit(solution)/shard_map/inner/pallas_call | solution.py:226
  30.2 0.0 collective-permute-done.far_ref
  30.2 0.0 copy-start.1
  30.2 2.3 %copy-done.1 = bf16[3,3,512,512]{3,2,1,0:T(8,128)(2,1)S(1)} copy-done((bf16[3,3,512,512]{3,2,1,0:T(8,128)(2,1)S(1)}, bf16[3,3,512,512]{3,2,1,0:T(8,128)(2,1)}, u32[]{:S(2)}) %copy-start.1) | copy-done | bytes 4718616
  32.5 2.6 %outer.1 = bf16[256,512]{1,0:T(8,128)(2,1)} custom-call(s32[2]{0:T(128)S(1)} %pad_add_fusion.meta_ref, bf16[272,512]{1,0:T(8,128)(2,1)S(1)} %collective-permute-done.far_ref, bf16[16,2,8,512]{3,2,1,0:T(8,128)(2,1)S(1)} %all-to-all-done.same_ref, bf16[16,2,8,512]{3,2,1,0:T(8,128)(2,1)S(1)} %collective-permute-done.1.other_ref, ...), custom_call_target="tpu_custom_call" | custom-call | flops 603979776 | bytes 2359296 | tf_op jit(solution)/shard_map/outer/pallas_call | solution.py:245
  (6 shorter events, 0.1 us)
Async XLA Ops:
  1.5 16.8 %all-to-all-start = ((bf16[16,2,8,512]{3,2,1,0:T(8,128)(2,1)}), bf16[16,2,8,512]{3,2,1,0:T(8,128)(2,1)S(1)}, u32[]{:S(2)}, u32[]{:S(2)}) async-start(bf16[16,2,8,512]{3,2,1,0:T(8,128)(2,1)} %broadcast_in_dim.36), calls=%async_computation | async-start | bytes 524288 | tf_op jit(solution)/shard_map/all_to_all | solution.py:187
  12.0 9.6 %copy-start.4 = (bf16[512,512]{1,0:T(8,128)(2,1)S(1)}, bf16[512,512]{1,0:T(8,128)(2,1)}, u32[]{:S(2)}) copy-start(bf16[512,512]{1,0:T(8,128)(2,1)} %param.14) | copy-start | bytes 1572868
  14.0 7.6 %collective-permute-start.2 = (bf16[272,512]{1,0:T(8,128)(2,1)}, bf16[272,512]{1,0:T(8,128)(2,1)S(1)}, u32[]{:S(2)}, u32[]{:S(2)}) collective-permute-start(bf16[272,512]{1,0:T(8,128)(2,1)} %get-tuple-element.25.near_sent_ref), channel_id=1, source_target_pairs={{0,1},{1,0},{2,3},{3,2},{4,5},{5,4},{6,7},{7,6},{8,9},{9,8},{10,11... | collective-permute-start | bytes 835592 | tf_op jit(solution)/shard_map/ppermute | solution.py:214
  15.2 14.9 %collective-permute-start = (bf16[272,512]{1,0:T(8,128)(2,1)}, bf16[272,512]{1,0:T(8,128)(2,1)S(1)}, u32[]{:S(2)}, u32[]{:S(2)}) collective-permute-start(bf16[272,512]{1,0:T(8,128)(2,1)} %get-tuple-element.21.far_sent_ref), channel_id=1, source_target_pairs={{1,2},{3,4},{5,6},{7,8},{9,10},{11,12},{13,14},{15,16},{17,18},{19... | collective-permute-start | bytes 835592 | tf_op jit(solution)/shard_map/ppermute | solution.py:213
  18.2 4.4 %collective-permute-start.1 = (bf16[16,2,8,512]{3,2,1,0:T(8,128)(2,1)S(1)}, bf16[16,2,8,512]{3,2,1,0:T(8,128)(2,1)S(1)}, u32[]{:S(2)}, u32[]{:S(2)}) collective-permute-start(bf16[16,2,8,512]{3,2,1,0:T(8,128)(2,1)S(1)} %all-to-all-done.same_ref), channel_id=1, source_target_pairs={{0,1},{1,0},{2,3},{3,2},{4,5},{5,4},{6,7},{7,6},{8,9},{9,8},{10,11... | collective-permute-start | bytes 786440 | tf_op jit(solution)/shard_map/ppermute | solution.py:215
  22.7 2.3 %copy-start = (bf16[3,3,512,512]{3,2,1,0:T(8,128)(2,1)S(1)}, bf16[3,3,512,512]{3,2,1,0:T(8,128)(2,1)}, u32[]{:S(2)}) copy-start(bf16[3,3,512,512]{3,2,1,0:T(8,128)(2,1)} %conv_ref.3) | copy-start | bytes 14155780
  25.0 1.0 %copy-start.2 = (bf16[272,512]{1,0:T(8,128)(2,1)S(1)}, bf16[272,512]{1,0:T(8,128)(2,1)}, u32[]{:S(2)}) copy-start(bf16[272,512]{1,0:T(8,128)(2,1)} %get-tuple-element.21.far_sent_ref) | copy-start | bytes 835588
  26.0 1.0 %copy-start.3 = (bf16[272,512]{1,0:T(8,128)(2,1)S(1)}, bf16[272,512]{1,0:T(8,128)(2,1)}, u32[]{:S(2)}) copy-start(bf16[272,512]{1,0:T(8,128)(2,1)} %get-tuple-element.25.near_sent_ref) | copy-start | bytes 835588
  30.2 2.3 %copy-start.1 = (bf16[3,3,512,512]{3,2,1,0:T(8,128)(2,1)S(1)}, bf16[3,3,512,512]{3,2,1,0:T(8,128)(2,1)}, u32[]{:S(2)}) copy-start(bf16[3,3,512,512]{3,2,1,0:T(8,128)(2,1)} %conv_ref.3) | copy-start | bytes 14155780

commit v7 on v6

--- a/solution.py
+++ b/solution.py
@@ -207,7 +207,8 @@
         out_shape=[payload] * 2,
         in_specs=[vmem] * 6,
         out_specs=[vmem] * 2,
-        cost_estimate=pl.CostEstimate(flops=10**10, bytes_accessed=4 * payload.size * 2, transcendentals=0),
+        compiler_params=pltpu.CompilerParams(vmem_limit_bytes=4 * 2**20),
+        cost_estimate=pl.CostEstimate(flops=10**10, bytes_accessed=8 * payload.size, transcendentals=0),
         name="pack",
     )(*query_rows, *grid_rows, *limit_rows)
     far = lax.ppermute(far_sent, AXES, across)

time: 35.6 us -> 32.9 us (0.924)
  the two profiles are of different devices: /device:TPU:5 before, /device:TPU:0 now
where the time goes in v7:
time: 32.9 us; the launch traced here: 32.6 us
  waiting for transfers between devices  9.36 us (28%)
  starting transfers between devices  9.06 us (28%)
  local copies, waits for them, and re-layouts  6.61 us (20%)
  Pallas kernels  5.92 us (18%)
  other arithmetic  1.48 us (4%)
    all_to_all x1, starting transfers between devices, on_device(): lax.all_to_all(jnp.broadcast_to(block[None], (pairs,) + block.shape), AXE...  8.31 us
    all_to_all x1, waiting for transfers between devices, on_device(): lax.all_to_all(jnp.broadcast_to(block[None], (pairs,) + block.shape), AXE...  7.95 us
    unnamed x6, local copies, waits for them, and re-layouts  4.68 us
    pallas_call x1, Pallas kernels, on_device(): pl.pallas_call(functools.partial(inner_kernel, *sizes), out_shape=[jax.Sh...  3.23 us
    pallas_call x1, Pallas kernels, on_device(): pl.pallas_call(functools.partial(outer_kernel, *sizes), out_shape=jax.Sha...  2.63 us
    ppermute x1, waiting for transfers between devices, on_device(): other = lax.ppermute(same, AXES, swap)  1.4 us
    split x1, local copies, waits for them, and re-layouts, on_device(): jnp.split(grid_feat, tiles, axis=0)  1.13 us
    broadcast_in_dim x1, local copies, waits for them, and re-layouts, on_device(): jnp.broadcast_to(block[None], (pairs,) + block.shape)  0.73 us
  transfers between devices with their start and end apart: 4, of which 2 were waited for; matrix products, arithmetic and copies ran while one was open for 6% of the time, Pallas kernels for 10%

profile of v7, /device:TPU:0, one launch (start us, length us, event | category | flops | bytes accessed | tf_op | source)
XLA Modules:
  0.0 32.6 jit_solution(3958878760273958321)
XLA Ops:
  0.0 0.7 %pad_maximum_fusion = bf16[2,8,512]{2,1,0:T(8,128)(2,1)S(1)} fusion(bf16[1,8,512]{2,1,0:T(8,128)(2,1)} %bitcast.4, bf16[1,8,512]{2,1,0:T(8,128)(2,1)} %bitcast.5), kind=kLoop, calls=%fused_computation | loop fusion | flops 8192 | bytes 32768 | tf_op jit(solution)/shard_map/stack | solution.py:185
  0.7 0.7 %broadcast_in_dim.36 = bf16[16,2,8,512]{3,2,1,0:T(8,128)(2,1)} broadcast(bf16[2,8,512]{2,1,0:T(8,128)(2,1)S(1)} %pad_maximum_fusion), dimensions={1,2,3} | broadcast | bytes 278528 | tf_op jit(solution)/shard_map/broadcast_in_dim | solution.py:188
  1.5 8.3 %all-to-all-start = ((bf16[16,2,8,512]{3,2,1,0:T(8,128)(2,1)}), bf16[16,2,8,512]{3,2,1,0:T(8,128)(2,1)S(1)}, u32[]{:S(2)}, u32[]{:S(2)}) async-start(bf16[16,2,8,512]{3,2,1,0:T(8,128)(2,1)} %broadcast_in_dim.36), calls=%async_computation | async-start | bytes 524288 | tf_op jit(solution)/shard_map/all_to_all | solution.py:187
  9.8 1.1 %fusion.2 = (bf16[128,512]{1,0:T(8,128)(2,1)S(1)}, bf16[128,512]{1,0:T(8,128)(2,1)S(1)}, bf16[128,512]{1,0:T(8,128)(2,1)S(1)}, bf16[128,512]{1,0:T(8,128)(2,1)S(1)}) fusion(bf16[256,512]{1,0:T(8,128)(2,1)} %param.8, bf16[256,512]{1,0:T(8,128)(2,1)} %param.9), kind=kLoop, calls=%fused_computation.7 | loop fusion | bytes 1048576 | tf_op jit(solution)/shard_map/split | solution.py:195
  10.9 0.7 %fusion = bf16[2,2]{1,0:T(2,128)(2,1)S(1)} fusion(s32[2,2]{1,0:T(2,128)} %param.12, s32[2]{0:T(128)} %param.13), kind=kLoop, calls=%fused_computation.4 | loop fusion | flops 12 | bytes 32 | tf_op jit(solution)/shard_map/convert_element_type | solution.py:197
  11.6 0.0 copy-start.2
  11.7 0.1 pack.1
  11.7 0.1 collective-permute-start.2
  11.8 0.7 %collective-permute-start = (bf16[272,512]{1,0:T(8,128)(2,1)S(1)}, bf16[272,512]{1,0:T(8,128)(2,1)S(1)}, u32[]{:S(2)}, u32[]{:S(2)}) collective-permute-start(bf16[272,512]{1,0:T(8,128)(2,1)S(1)} %get-tuple-element.21.far_sent_ref), channel_id=1, source_target_pairs={{1,2},{3,4},{5,6},{7,8},{9,10},{11,12},{13,14},{15,16},{17,18},{19... | collective-permute-start | bytes 835592 | tf_op jit(solution)/shard_map/ppermute | solution.py:214
  12.5 7.9 %all-to-all-done.same_ref = bf16[16,2,8,512]{3,2,1,0:T(8,128)(2,1)S(1)} async-done(((bf16[16,2,8,512]{3,2,1,0:T(8,128)(2,1)}), bf16[16,2,8,512]{3,2,1,0:T(8,128)(2,1)S(1)}, u32[]{:S(2)}, u32[]{:S(2)}) %all-to-all-start) | async-done | bytes 262176 | tf_op jit(solution)/shard_map/all_to_all | solution.py:187
  20.5 0.0 collective-permute-start.1
  20.5 0.1 pad_add_fusion.meta_ref
  20.5 0.0 copy-done.2
  20.6 0.0 collective-permute-done.2.near_ref
  20.6 1.4 %collective-permute-done.1.other_ref = bf16[16,2,8,512]{3,2,1,0:T(8,128)(2,1)S(1)} collective-permute-done((bf16[16,2,8,512]{3,2,1,0:T(8,128)(2,1)S(1)}, bf16[16,2,8,512]{3,2,1,0:T(8,128)(2,1)S(1)}, u32[]{:S(2)}, u32[]{:S(2)}) %collective-permute-start.1) | collective-permute-done | bytes 262176 | tf_op jit(solution)/shard_map/ppermute | solution.py:216
  22.0 0.0 copy-start
  22.0 2.3 %copy-done = bf16[3,3,512,512]{3,2,1,0:T(8,128)(2,1)S(1)} copy-done((bf16[3,3,512,512]{3,2,1,0:T(8,128)(2,1)S(1)}, bf16[3,3,512,512]{3,2,1,0:T(8,128)(2,1)}, u32[]{:S(2)}) %copy-start) | copy-done | bytes 4718616
  24.3 3.2 %inner.1 = (bf16[128,512]{1,0:T(8,128)(2,1)S(1)}, f32[256,512]{1,0:T(8,128)S(1)}, bf16[512,256]{1,0:T(8,128)(2,1)S(1)}) custom-call(s32[2]{0:T(128)S(1)} %pad_add_fusion.meta_ref, bf16[272,512]{1,0:T(8,128)(2,1)S(1)} %collective-permute-done.2.near_ref, bf16[272,512]{1,0:T(8,128)(2,1)S(1)} %get-tuple-element.25.near_sent_ref, ...), custom_call_target="tpu_custom_call" | custom-call | flops 1409286144 | bytes 4718592 | tf_op jit(solution)/shard_map/inner/pallas_call | solution.py:227
  27.6 0.0 collective-permute-done.far_ref
  27.6 0.0 copy-start.1
  27.6 2.3 %copy-done.1 = bf16[3,3,512,512]{3,2,1,0:T(8,128)(2,1)S(1)} copy-done((bf16[3,3,512,512]{3,2,1,0:T(8,128)(2,1)S(1)}, bf16[3,3,512,512]{3,2,1,0:T(8,128)(2,1)}, u32[]{:S(2)}) %copy-start.1) | copy-done | bytes 4718616
  29.9 2.6 %outer.1 = bf16[256,512]{1,0:T(8,128)(2,1)} custom-call(s32[2]{0:T(128)S(1)} %pad_add_fusion.meta_ref, bf16[272,512]{1,0:T(8,128)(2,1)S(1)} %collective-permute-done.far_ref, bf16[16,2,8,512]{3,2,1,0:T(8,128)(2,1)S(1)} %all-to-all-done.same_ref, bf16[16,2,8,512]{3,2,1,0:T(8,128)(2,1)S(1)} %collective-permute-done.1.other_ref, ...), custom_call_target="tpu_custom_call" | custom-call | flops 603979776 | bytes 2359296 | tf_op jit(solution)/shard_map/outer/pallas_call | solution.py:246
  (4 shorter events, 0.1 us)
Async XLA Ops:
  1.5 19.0 %all-to-all-start = ((bf16[16,2,8,512]{3,2,1,0:T(8,128)(2,1)}), bf16[16,2,8,512]{3,2,1,0:T(8,128)(2,1)S(1)}, u32[]{:S(2)}, u32[]{:S(2)}) async-start(bf16[16,2,8,512]{3,2,1,0:T(8,128)(2,1)} %broadcast_in_dim.36), calls=%async_computation | async-start | bytes 524288 | tf_op jit(solution)/shard_map/all_to_all | solution.py:187
  11.6 8.9 %copy-start.2 = (bf16[512,512]{1,0:T(8,128)(2,1)S(1)}, bf16[512,512]{1,0:T(8,128)(2,1)}, u32[]{:S(2)}) copy-start(bf16[512,512]{1,0:T(8,128)(2,1)} %param.14) | copy-start | bytes 1572868
  11.7 8.9 %collective-permute-start.2 = (bf16[272,512]{1,0:T(8,128)(2,1)S(1)}, bf16[272,512]{1,0:T(8,128)(2,1)S(1)}, u32[]{:S(2)}, u32[]{:S(2)}) collective-permute-start(bf16[272,512]{1,0:T(8,128)(2,1)S(1)} %get-tuple-element.25.near_sent_ref), channel_id=1, source_target_pairs={{0,1},{1,0},{2,3},{3,2},{4,5},{5,4},{6,7},{7,6},{8,9},{9,8},{10,11... | collective-permute-start | bytes 835592 | tf_op jit(solution)/shard_map/ppermute | solution.py:215
  11.8 15.8 %collective-permute-start = (bf16[272,512]{1,0:T(8,128)(2,1)S(1)}, bf16[272,512]{1,0:T(8,128)(2,1)S(1)}, u32[]{:S(2)}, u32[]{:S(2)}) collective-permute-start(bf16[272,512]{1,0:T(8,128)(2,1)S(1)} %get-tuple-element.21.far_sent_ref), channel_id=1, source_target_pairs={{1,2},{3,4},{5,6},{7,8},{9,10},{11,12},{13,14},{15,16},{17,18},{19... | collective-permute-start | bytes 835592 | tf_op jit(solution)/shard_map/ppermute | solution.py:214
  20.5 1.5 %collective-permute-start.1 = (bf16[16,2,8,512]{3,2,1,0:T(8,128)(2,1)S(1)}, bf16[16,2,8,512]{3,2,1,0:T(8,128)(2,1)S(1)}, u32[]{:S(2)}, u32[]{:S(2)}) collective-permute-start(bf16[16,2,8,512]{3,2,1,0:T(8,128)(2,1)S(1)} %all-to-all-done.same_ref), channel_id=1, source_target_pairs={{0,1},{1,0},{2,3},{3,2},{4,5},{5,4},{6,7},{7,6},{8,9},{9,8},{10,11... | collective-permute-start | bytes 786440 | tf_op jit(solution)/shard_map/ppermute | solution.py:216
  22.0 2.3 %copy-start = (bf16[3,3,512,512]{3,2,1,0:T(8,128)(2,1)S(1)}, bf16[3,3,512,512]{3,2,1,0:T(8,128)(2,1)}, u32[]{:S(2)}) copy-start(bf16[3,3,512,512]{3,2,1,0:T(8,128)(2,1)} %conv_ref.3) | copy-start | bytes 14155780
  27.6 2.3 %copy-start.1 = (bf16[3,3,512,512]{3,2,1,0:T(8,128)(2,1)S(1)}, bf16[3,3,512,512]{3,2,1,0:T(8,128)(2,1)}, u32[]{:S(2)}) copy-start(bf16[3,3,512,512]{3,2,1,0:T(8,128)(2,1)} %conv_ref.3) | copy-start | bytes 14155780

commit v8 on v7

--- a/solution.py
+++ b/solution.py
@@ -107,9 +107,16 @@
 def inner_kernel(
     lon, width, nblocks, rows,
     meta_ref, near_ref, near_sent_ref, far_sent_ref, same_ref, other_ref, upper_ref, lower_ref,
-    conv_ref, edge_ref, partial_ref, keys_ref, mixed_ref, field_ref,
+    conv_hbm, edge_ref, partial_ref, keys_ref, last_ref, conv_ref, mixed_ref, field_ref, sems,
 ):
     core = meta_ref[0]
+    copies = [
+        pltpu.make_async_copy(conv_hbm.at[source], conv_ref.at[i], sems.at[i])
+        for i, source in enumerate((1, 2 - 2 * core))
+    ]
+    copies.append(pltpu.make_async_copy(conv_hbm.at[2 * core], last_ref, sems.at[2]))
+    for copy in copies:
+        copy.start()
 
     def keys_of(cols):
         keys = both_cores(same_ref, other_ref, 0, cols).T
@@ -124,13 +131,16 @@
     edge_ref[...] = field_ref[2 * lon :, :]
     inputs = jnp.concatenate([field_ref[lon:, :], field_ref[: 2 * lon, :]], axis=1)
     terms = []
+    copies[0].wait()
+    copies[1].wait()
     for lon_off in range(3):
-        taps = jnp.concatenate([conv_ref[1, lon_off], conv_ref[2 - 2 * core, lon_off]], axis=0)
+        taps = conv_ref[:, lon_off].reshape(2 * width, width)
         terms.append(jnp.dot(inputs, taps, preferred_element_type=jnp.float32))
     for start in (0, lon):
         here = slice(start, start + lon)
         shifted = around([term[here] for term in terms], lon)
         partial_ref[here, :] = wide[start + lon : start + 2 * lon] + shifted
+    copies[2].wait()
 
 
 def outer_kernel(
@@ -146,8 +156,7 @@
     far = jnp.where(meta_ref[1] > 0, normed, 0.0).astype(jnp.bfloat16)
     field = jnp.concatenate([edge_ref[...], far], axis=0)
     terms = [
-        jnp.dot(field, conv_ref[2 * core, lon_off], preferred_element_type=jnp.float32)
-        for lon_off in range(3)
+        jnp.dot(field, conv_ref[lon_off], preferred_element_type=jnp.float32) for lon_off in range(3)
     ]
     for start, tile in ((0, 1 - core), (lon, core)):
         here = slice(start, start + lon)
@@ -221,21 +230,25 @@
     meta = jnp.stack([core, far_exists.astype(core.dtype)]).astype(jnp.int32)
 
     smem = pl.BlockSpec(memory_space=pltpu.SMEM)
+    hbm = pl.BlockSpec(memory_space=pltpu.HBM)
     sizes = (lon, width, nblocks, rows)
-    params = pltpu.CompilerParams(vmem_limit_bytes=40 * 2**20)
+    params = pltpu.CompilerParams(vmem_limit_bytes=48 * 2**20)
     tap_flops, row_flops = 2 * lon * width * width, 2 * lon * width * (width + 4 * obs)
-    edge, partial, keys = pl.pallas_call(
+    edge, partial, keys, taps = pl.pallas_call(
         functools.partial(inner_kernel, *sizes),
         out_shape=[
             jax.ShapeDtypeStruct((lon, width), jnp.bfloat16),
             jax.ShapeDtypeStruct((q_dev, width), jnp.float32),
             jax.ShapeDtypeStruct((width, obs), jnp.bfloat16),
+            jax.ShapeDtypeStruct(conv_weight.shape[1:], jnp.bfloat16),
         ],
-        in_specs=[smem] + [vmem] * 8,
-        out_specs=[vmem] * 3,
+        in_specs=[smem] + [vmem] * 7 + [hbm],
+        out_specs=[vmem] * 4,
         scratch_shapes=[
+            pltpu.VMEM((2,) + conv_weight.shape[1:], jnp.bfloat16),
             pltpu.VMEM((3 * lon, width), jnp.bfloat16),
             pltpu.VMEM((3 * lon, width), jnp.bfloat16),
+            pltpu.SemaphoreType.DMA((3,)),
         ],
         compiler_params=params,
         cost_estimate=pl.CostEstimate(
@@ -256,7 +269,7 @@
             flops=row_flops + 6 * tap_flops, bytes_accessed=conv_weight.size, transcendentals=0
         ),
         name="outer",
-    )(meta, far, same, other, upper, lower, edge, partial, keys, conv_weight)
+    )(meta, far, same, other, upper, lower, edge, partial, keys, taps)
 
 
 def solution(mesh):

time: 32.9 us -> 29.7 us (0.903)
  local copies, waits for them, and re-layouts: 6.61 us -> 1.94 us
  Pallas kernels: 5.92 us -> 7.37 us
    unnamed x6 -> x2, local copies, waits for them, and re-layouts: 4.68 us -> 0.01 us
    pallas_call x1, Pallas kernels: 3.23 us -> 4.68 us  [on_device(): pl.pallas_call(functools.partial(inner_kernel, *sizes), out_shape=[jax.Sh...]
  transfers between devices with their start and end apart: 4 -> 4, of which waited for: 2 -> 2; matrix products, arithmetic and copies ran while one was open for 6% -> 7% of each run, Pallas kernels for 10% -> 16%
where the time goes in v8:
time: 29.7 us; the launch traced here: 29.3 us
  waiting for transfers between devices  9.36 us (32%)
  starting transfers between devices  9.06 us (31%)
  Pallas kernels  7.37 us (25%)
  local copies, waits for them, and re-layouts  1.94 us (7%)
  other arithmetic  1.48 us (5%)
    all_to_all x1, starting transfers between devices, on_device(): lax.all_to_all(jnp.broadcast_to(block[None], (pairs,) + block.shape), AXE...  8.31 us
    all_to_all x1, waiting for transfers between devices, on_device(): lax.all_to_all(jnp.broadcast_to(block[None], (pairs,) + block.shape), AXE...  7.95 us
    pallas_call x1, Pallas kernels, on_device(): pl.pallas_call(functools.partial(inner_kernel, *sizes), out_shape=[jax.Sh...  4.68 us
    pallas_call x1, Pallas kernels, on_device(): pl.pallas_call(functools.partial(outer_kernel, *sizes), out_shape=jax.Sha...  2.64 us
    ppermute x1, waiting for transfers between devices, on_device(): other = lax.ppermute(same, AXES, swap)  1.4 us
    split x1, local copies, waits for them, and re-layouts, on_device(): jnp.split(grid_feat, tiles, axis=0)  1.13 us
    broadcast_in_dim x1, local copies, waits for them, and re-layouts, on_device(): jnp.broadcast_to(block[None], (pairs,) + block.shape)  0.73 us
    another operation x1, other arithmetic, on_device(): block = jnp.stack([obs_keys, obs_values])  0.72 us
  transfers between devices with their start and end apart: 4, of which 2 were waited for; matrix products, arithmetic and copies ran while one was open for 7% of the time, Pallas kernels for 16%

profile of v8, /device:TPU:0, one launch (start us, length us, event | category | flops | bytes accessed | tf_op | source)
XLA Modules:
  0.0 29.3 jit_solution(11497506447747046181)
XLA Ops:
  0.0 0.7 %pad_maximum_fusion = bf16[2,8,512]{2,1,0:T(8,128)(2,1)S(1)} fusion(bf16[1,8,512]{2,1,0:T(8,128)(2,1)} %bitcast.4, bf16[1,8,512]{2,1,0:T(8,128)(2,1)} %bitcast.5), kind=kLoop, calls=%fused_computation | loop fusion | flops 8192 | bytes 32768 | tf_op jit(solution)/shard_map/stack | solution.py:194
  0.7 0.7 %broadcast_in_dim.36 = bf16[16,2,8,512]{3,2,1,0:T(8,128)(2,1)} broadcast(bf16[2,8,512]{2,1,0:T(8,128)(2,1)S(1)} %pad_maximum_fusion), dimensions={1,2,3} | broadcast | bytes 278528 | tf_op jit(solution)/shard_map/broadcast_in_dim | solution.py:197
  1.5 8.3 %all-to-all-start = ((bf16[16,2,8,512]{3,2,1,0:T(8,128)(2,1)}), bf16[16,2,8,512]{3,2,1,0:T(8,128)(2,1)S(1)}, u32[]{:S(2)}, u32[]{:S(2)}) async-start(bf16[16,2,8,512]{3,2,1,0:T(8,128)(2,1)} %broadcast_in_dim.36), calls=%async_computation | async-start | bytes 524288 | tf_op jit(solution)/shard_map/all_to_all | solution.py:196
  9.8 1.1 %fusion.2 = (bf16[128,512]{1,0:T(8,128)(2,1)S(1)}, bf16[128,512]{1,0:T(8,128)(2,1)S(1)}, bf16[128,512]{1,0:T(8,128)(2,1)S(1)}, bf16[128,512]{1,0:T(8,128)(2,1)S(1)}) fusion(bf16[256,512]{1,0:T(8,128)(2,1)} %param.8, bf16[256,512]{1,0:T(8,128)(2,1)} %param.9), kind=kLoop, calls=%fused_computation.7 | loop fusion | bytes 1048576 | tf_op jit(solution)/shard_map/split | solution.py:204
  10.9 0.7 %fusion = bf16[2,2]{1,0:T(2,128)(2,1)S(1)} fusion(s32[2,2]{1,0:T(2,128)} %param.12, s32[2]{0:T(128)} %param.13), kind=kLoop, calls=%fused_computation.4 | loop fusion | flops 12 | bytes 32 | tf_op jit(solution)/shard_map/convert_element_type | solution.py:206
  11.6 0.0 copy-start
  11.7 0.1 pack.1
  11.7 0.1 collective-permute-start.2
  11.8 0.7 %collective-permute-start = (bf16[272,512]{1,0:T(8,128)(2,1)S(1)}, bf16[272,512]{1,0:T(8,128)(2,1)S(1)}, u32[]{:S(2)}, u32[]{:S(2)}) collective-permute-start(bf16[272,512]{1,0:T(8,128)(2,1)S(1)} %get-tuple-element.22.far_sent_ref), channel_id=1, source_target_pairs={{1,2},{3,4},{5,6},{7,8},{9,10},{11,12},{13,14},{15,16},{17,18},{19... | collective-permute-start | bytes 835592 | tf_op jit(solution)/shard_map/ppermute | solution.py:223
  12.5 7.9 %all-to-all-done.same_ref = bf16[16,2,8,512]{3,2,1,0:T(8,128)(2,1)S(1)} async-done(((bf16[16,2,8,512]{3,2,1,0:T(8,128)(2,1)}), bf16[16,2,8,512]{3,2,1,0:T(8,128)(2,1)S(1)}, u32[]{:S(2)}, u32[]{:S(2)}) %all-to-all-start) | async-done | bytes 262176 | tf_op jit(solution)/shard_map/all_to_all | solution.py:196
  20.5 0.0 collective-permute-start.1
  20.5 0.1 pad_add_fusion.meta_ref
  20.5 0.0 copy-done
  20.6 0.0 collective-permute-done.2.near_ref
  20.6 1.4 %collective-permute-done.1.other_ref = bf16[16,2,8,512]{3,2,1,0:T(8,128)(2,1)S(1)} collective-permute-done((bf16[16,2,8,512]{3,2,1,0:T(8,128)(2,1)S(1)}, bf16[16,2,8,512]{3,2,1,0:T(8,128)(2,1)S(1)}, u32[]{:S(2)}, u32[]{:S(2)}) %collective-permute-start.1) | collective-permute-done | bytes 262176 | tf_op jit(solution)/shard_map/ppermute | solution.py:225
  22.0 4.7 %inner.1 = (bf16[128,512]{1,0:T(8,128)(2,1)S(1)}, f32[256,512]{1,0:T(8,128)S(1)}, bf16[512,256]{1,0:T(8,128)(2,1)S(1)}, bf16[3,512,512]{2,1,0:T(8,128)(2,1)S(1)}) custom-call(s32[2]{0:T(128)S(1)} %pad_add_fusion.meta_ref, bf16[272,512]{1,0:T(8,128)(2,1)S(1)} %collective-permute-done.2.near_ref, bf16[272,512]{1,0:T(8,128)(2,1)S(1)} %get-tuple-element.26.near_sent_ref, ...), custom_call_target="tpu_custom_call" | custom-call | flops 1409286144 | bytes 4718592 | tf_op jit(solution)/shard_map/inner/pallas_call | solution.py:237
  26.7 0.0 collective-permute-done.far_ref
  26.7 2.6 %outer.1 = bf16[256,512]{1,0:T(8,128)(2,1)} custom-call(s32[2]{0:T(128)S(1)} %pad_add_fusion.meta_ref, bf16[272,512]{1,0:T(8,128)(2,1)S(1)} %collective-permute-done.far_ref, bf16[16,2,8,512]{3,2,1,0:T(8,128)(2,1)S(1)} %all-to-all-done.same_ref, bf16[16,2,8,512]{3,2,1,0:T(8,128)(2,1)S(1)} %collective-permute-done.1.other_ref, ...), custom_call_target="tpu_custom_call" | custom-call | flops 603979776 | bytes 2359296 | tf_op jit(solution)/shard_map/outer/pallas_call | solution.py:259
  (4 shorter events, 0.1 us)
Async XLA Ops:
  1.5 19.0 %all-to-all-start = ((bf16[16,2,8,512]{3,2,1,0:T(8,128)(2,1)}), bf16[16,2,8,512]{3,2,1,0:T(8,128)(2,1)S(1)}, u32[]{:S(2)}, u32[]{:S(2)}) async-start(bf16[16,2,8,512]{3,2,1,0:T(8,128)(2,1)} %broadcast_in_dim.36), calls=%async_computation | async-start | bytes 524288 | tf_op jit(solution)/shard_map/all_to_all | solution.py:196
  11.6 8.9 %copy-start = (bf16[512,512]{1,0:T(8,128)(2,1)S(1)}, bf16[512,512]{1,0:T(8,128)(2,1)}, u32[]{:S(2)}) copy-start(bf16[512,512]{1,0:T(8,128)(2,1)} %param.14) | copy-start | bytes 1572868
  11.7 8.9 %collective-permute-start.2 = (bf16[272,512]{1,0:T(8,128)(2,1)S(1)}, bf16[272,512]{1,0:T(8,128)(2,1)S(1)}, u32[]{:S(2)}, u32[]{:S(2)}) collective-permute-start(bf16[272,512]{1,0:T(8,128)(2,1)S(1)} %get-tuple-element.26.near_sent_ref), channel_id=1, source_target_pairs={{0,1},{1,0},{2,3},{3,2},{4,5},{5,4},{6,7},{7,6},{8,9},{9,8},{10,11... | collective-permute-start | bytes 835592 | tf_op jit(solution)/shard_map/ppermute | solution.py:224
  11.8 14.9 %collective-permute-start = (bf16[272,512]{1,0:T(8,128)(2,1)S(1)}, bf16[272,512]{1,0:T(8,128)(2,1)S(1)}, u32[]{:S(2)}, u32[]{:S(2)}) collective-permute-start(bf16[272,512]{1,0:T(8,128)(2,1)S(1)} %get-tuple-element.22.far_sent_ref), channel_id=1, source_target_pairs={{1,2},{3,4},{5,6},{7,8},{9,10},{11,12},{13,14},{15,16},{17,18},{19... | collective-permute-start | bytes 835592 | tf_op jit(solution)/shard_map/ppermute | solution.py:223
  20.5 1.5 %collective-permute-start.1 = (bf16[16,2,8,512]{3,2,1,0:T(8,128)(2,1)S(1)}, bf16[16,2,8,512]{3,2,1,0:T(8,128)(2,1)S(1)}, u32[]{:S(2)}, u32[]{:S(2)}) collective-permute-start(bf16[16,2,8,512]{3,2,1,0:T(8,128)(2,1)S(1)} %all-to-all-done.same_ref), channel_id=1, source_target_pairs={{0,1},{1,0},{2,3},{3,2},{4,5},{5,4},{6,7},{7,6},{8,9},{9,8},{10,11... | collective-permute-start | bytes 786440 | tf_op jit(solution)/shard_map/ppermute | solution.py:225

commit v9 on v8

--- a/solution.py
+++ b/solution.py
@@ -111,10 +111,13 @@
 ):
     core = meta_ref[0]
     copies = [
-        pltpu.make_async_copy(conv_hbm.at[source], conv_ref.at[i], sems.at[i])
+        pltpu.make_async_copy(
+            conv_hbm.at[source, lon_off], conv_ref.at[i, lon_off], sems.at[2 * lon_off + i]
+        )
+        for lon_off in range(3)
         for i, source in enumerate((1, 2 - 2 * core))
     ]
-    copies.append(pltpu.make_async_copy(conv_hbm.at[2 * core], last_ref, sems.at[2]))
+    copies.append(pltpu.make_async_copy(conv_hbm.at[2 * core], last_ref, sems.at[6]))
     for copy in copies:
         copy.start()
 
@@ -131,16 +134,16 @@
     edge_ref[...] = field_ref[2 * lon :, :]
     inputs = jnp.concatenate([field_ref[lon:, :], field_ref[: 2 * lon, :]], axis=1)
     terms = []
-    copies[0].wait()
-    copies[1].wait()
     for lon_off in range(3):
+        for copy in copies[2 * lon_off : 2 * lon_off + 2]:
+            copy.wait()
         taps = conv_ref[:, lon_off].reshape(2 * width, width)
         terms.append(jnp.dot(inputs, taps, preferred_element_type=jnp.float32))
     for start in (0, lon):
         here = slice(start, start + lon)
         shifted = around([term[here] for term in terms], lon)
         partial_ref[here, :] = wide[start + lon : start + 2 * lon] + shifted
-    copies[2].wait()
+    copies[6].wait()
 
 
 def outer_kernel(
@@ -248,7 +251,7 @@
             pltpu.VMEM((2,) + conv_weight.shape[1:], jnp.bfloat16),
             pltpu.VMEM((3 * lon, width), jnp.bfloat16),
             pltpu.VMEM((3 * lon, width), jnp.bfloat16),
-            pltpu.SemaphoreType.DMA((3,)),
+            pltpu.SemaphoreType.DMA((7,)),
         ],
         compiler_params=params,
         cost_estimate=pl.CostEstimate(

time: 29.7 us -> 29.4 us (0.990)
  Pallas kernels: 7.37 us -> 7.05 us
    pallas_call x1, Pallas kernels: 4.68 us -> 4.37 us  [on_device(): pl.pallas_call(functools.partial(inner_kernel, *sizes), out_shape=[jax.Sh...]
  transfers between devices with their start and end apart: 4 -> 4, of which waited for: 2 -> 2; matrix products, arithmetic and copies ran while one was open for 7% -> 7% of each run, Pallas kernels for 16% -> 15%
where the time goes in v9:
time: 29.4 us; the launch traced here: 29 us
  waiting for transfers between devices  9.36 us (32%)
  starting transfers between devices  9.06 us (31%)
  Pallas kernels  7.05 us (24%)
  local copies, waits for them, and re-layouts  1.94 us (7%)
  other arithmetic  1.48 us (5%)
    all_to_all x1, starting transfers between devices, on_device(): lax.all_to_all(jnp.broadcast_to(block[None], (pairs,) + block.shape), AXE...  8.31 us
    all_to_all x1, waiting for transfers between devices, on_device(): lax.all_to_all(jnp.broadcast_to(block[None], (pairs,) + block.shape), AXE...  7.95 us
    pallas_call x1, Pallas kernels, on_device(): pl.pallas_call(functools.partial(inner_kernel, *sizes), out_shape=[jax.Sh...  4.37 us
    pallas_call x1, Pallas kernels, on_device(): pl.pallas_call(functools.partial(outer_kernel, *sizes), out_shape=jax.Sha...  2.63 us
    ppermute x1, waiting for transfers between devices, on_device(): other = lax.ppermute(same, AXES, swap)  1.4 us
    split x1, local copies, waits for them, and re-layouts, on_device(): jnp.split(grid_feat, tiles, axis=0)  1.13 us
    broadcast_in_dim x1, local copies, waits for them, and re-layouts, on_device(): jnp.broadcast_to(block[None], (pairs,) + block.shape)  0.73 us
    another operation x1, other arithmetic, on_device(): block = jnp.stack([obs_keys, obs_values])  0.72 us
  transfers between devices with their start and end apart: 4, of which 2 were waited for; matrix products, arithmetic and copies ran while one was open for 7% of the time, Pallas kernels for 15%

profile of v9, /device:TPU:0, one launch (start us, length us, event | category | flops | bytes accessed | tf_op | source)
XLA Modules:
  0.0 29.0 jit_solution(7117315744690998990)
XLA Ops:
  0.0 0.7 %pad_maximum_fusion = bf16[2,8,512]{2,1,0:T(8,128)(2,1)S(1)} fusion(bf16[1,8,512]{2,1,0:T(8,128)(2,1)} %bitcast.4, bf16[1,8,512]{2,1,0:T(8,128)(2,1)} %bitcast.5), kind=kLoop, calls=%fused_computation | loop fusion | flops 8192 | bytes 32768 | tf_op jit(solution)/shard_map/stack | solution.py:197
  0.7 0.7 %broadcast_in_dim.36 = bf16[16,2,8,512]{3,2,1,0:T(8,128)(2,1)} broadcast(bf16[2,8,512]{2,1,0:T(8,128)(2,1)S(1)} %pad_maximum_fusion), dimensions={1,2,3} | broadcast | bytes 278528 | tf_op jit(solution)/shard_map/broadcast_in_dim | solution.py:200
  1.5 8.3 %all-to-all-start = ((bf16[16,2,8,512]{3,2,1,0:T(8,128)(2,1)}), bf16[16,2,8,512]{3,2,1,0:T(8,128)(2,1)S(1)}, u32[]{:S(2)}, u32[]{:S(2)}) async-start(bf16[16,2,8,512]{3,2,1,0:T(8,128)(2,1)} %broadcast_in_dim.36), calls=%async_computation | async-start | bytes 524288 | tf_op jit(solution)/shard_map/all_to_all | solution.py:199
  9.8 1.1 %fusion.2 = (bf16[128,512]{1,0:T(8,128)(2,1)S(1)}, bf16[128,512]{1,0:T(8,128)(2,1)S(1)}, bf16[128,512]{1,0:T(8,128)(2,1)S(1)}, bf16[128,512]{1,0:T(8,128)(2,1)S(1)}) fusion(bf16[256,512]{1,0:T(8,128)(2,1)} %param.8, bf16[256,512]{1,0:T(8,128)(2,1)} %param.9), kind=kLoop, calls=%fused_computation.7 | loop fusion | bytes 1048576 | tf_op jit(solution)/shard_map/split | solution.py:207
  10.9 0.7 %fusion = bf16[2,2]{1,0:T(2,128)(2,1)S(1)} fusion(s32[2,2]{1,0:T(2,128)} %param.12, s32[2]{0:T(128)} %param.13), kind=kLoop, calls=%fused_computation.4 | loop fusion | flops 12 | bytes 32 | tf_op jit(solution)/shard_map/convert_element_type | solution.py:209
  11.6 0.0 copy-start
  11.7 0.1 pack.1
  11.7 0.1 collective-permute-start.2
  11.8 0.7 %collective-permute-start = (bf16[272,512]{1,0:T(8,128)(2,1)S(1)}, bf16[272,512]{1,0:T(8,128)(2,1)S(1)}, u32[]{:S(2)}, u32[]{:S(2)}) collective-permute-start(bf16[272,512]{1,0:T(8,128)(2,1)S(1)} %get-tuple-element.22.far_sent_ref), channel_id=1, source_target_pairs={{1,2},{3,4},{5,6},{7,8},{9,10},{11,12},{13,14},{15,16},{17,18},{19... | collective-permute-start | bytes 835592 | tf_op jit(solution)/shard_map/ppermute | solution.py:226
  12.5 7.9 %all-to-all-done.same_ref = bf16[16,2,8,512]{3,2,1,0:T(8,128)(2,1)S(1)} async-done(((bf16[16,2,8,512]{3,2,1,0:T(8,128)(2,1)}), bf16[16,2,8,512]{3,2,1,0:T(8,128)(2,1)S(1)}, u32[]{:S(2)}, u32[]{:S(2)}) %all-to-all-start) | async-done | bytes 262176 | tf_op jit(solution)/shard_map/all_to_all | solution.py:199
  20.5 0.0 collective-permute-start.1
  20.5 0.1 pad_add_fusion.meta_ref
  20.5 0.0 copy-done
  20.6 0.0 collective-permute-done.2.near_ref
  20.6 1.4 %collective-permute-done.1.other_ref = bf16[16,2,8,512]{3,2,1,0:T(8,128)(2,1)S(1)} collective-permute-done((bf16[16,2,8,512]{3,2,1,0:T(8,128)(2,1)S(1)}, bf16[16,2,8,512]{3,2,1,0:T(8,128)(2,1)S(1)}, u32[]{:S(2)}, u32[]{:S(2)}) %collective-permute-start.1) | collective-permute-done | bytes 262176 | tf_op jit(solution)/shard_map/ppermute | solution.py:228
  22.0 4.4 %inner.1 = (bf16[128,512]{1,0:T(8,128)(2,1)S(1)}, f32[256,512]{1,0:T(8,128)S(1)}, bf16[512,256]{1,0:T(8,128)(2,1)S(1)}, bf16[3,512,512]{2,1,0:T(8,128)(2,1)S(1)}) custom-call(s32[2]{0:T(128)S(1)} %pad_add_fusion.meta_ref, bf16[272,512]{1,0:T(8,128)(2,1)S(1)} %collective-permute-done.2.near_ref, bf16[272,512]{1,0:T(8,128)(2,1)S(1)} %get-tuple-element.26.near_sent_ref, ...), custom_call_target="tpu_custom_call" | custom-call | flops 1409286144 | bytes 4718592 | tf_op jit(solution)/shard_map/inner/pallas_call | solution.py:240
  26.4 0.0 collective-permute-done.far_ref
  26.4 2.6 %outer.1 = bf16[256,512]{1,0:T(8,128)(2,1)} custom-call(s32[2]{0:T(128)S(1)} %pad_add_fusion.meta_ref, bf16[272,512]{1,0:T(8,128)(2,1)S(1)} %collective-permute-done.far_ref, bf16[16,2,8,512]{3,2,1,0:T(8,128)(2,1)S(1)} %all-to-all-done.same_ref, bf16[16,2,8,512]{3,2,1,0:T(8,128)(2,1)S(1)} %collective-permute-done.1.other_ref, ...), custom_call_target="tpu_custom_call" | custom-call | flops 603979776 | bytes 2359296 | tf_op jit(solution)/shard_map/outer/pallas_call | solution.py:262
  (4 shorter events, 0.1 us)
Async XLA Ops:
  1.5 19.0 %all-to-all-start = ((bf16[16,2,8,512]{3,2,1,0:T(8,128)(2,1)}), bf16[16,2,8,512]{3,2,1,0:T(8,128)(2,1)S(1)}, u32[]{:S(2)}, u32[]{:S(2)}) async-start(bf16[16,2,8,512]{3,2,1,0:T(8,128)(2,1)} %broadcast_in_dim.36), calls=%async_computation | async-start | bytes 524288 | tf_op jit(solution)/shard_map/all_to_all | solution.py:199
  11.6 8.9 %copy-start = (bf16[512,512]{1,0:T(8,128)(2,1)S(1)}, bf16[512,512]{1,0:T(8,128)(2,1)}, u32[]{:S(2)}) copy-start(bf16[512,512]{1,0:T(8,128)(2,1)} %param.14) | copy-start | bytes 1572868
  11.7 8.9 %collective-permute-start.2 = (bf16[272,512]{1,0:T(8,128)(2,1)S(1)}, bf16[272,512]{1,0:T(8,128)(2,1)S(1)}, u32[]{:S(2)}, u32[]{:S(2)}) collective-permute-start(bf16[272,512]{1,0:T(8,128)(2,1)S(1)} %get-tuple-element.26.near_sent_ref), channel_id=1, source_target_pairs={{0,1},{1,0},{2,3},{3,2},{4,5},{5,4},{6,7},{7,6},{8,9},{9,8},{10,11... | collective-permute-start | bytes 835592 | tf_op jit(solution)/shard_map/ppermute | solution.py:227
  11.8 14.6 %collective-permute-start = (bf16[272,512]{1,0:T(8,128)(2,1)S(1)}, bf16[272,512]{1,0:T(8,128)(2,1)S(1)}, u32[]{:S(2)}, u32[]{:S(2)}) collective-permute-start(bf16[272,512]{1,0:T(8,128)(2,1)S(1)} %get-tuple-element.22.far_sent_ref), channel_id=1, source_target_pairs={{1,2},{3,4},{5,6},{7,8},{9,10},{11,12},{13,14},{15,16},{17,18},{19... | collective-permute-start | bytes 835592 | tf_op jit(solution)/shard_map/ppermute | solution.py:226
  20.5 1.5 %collective-permute-start.1 = (bf16[16,2,8,512]{3,2,1,0:T(8,128)(2,1)S(1)}, bf16[16,2,8,512]{3,2,1,0:T(8,128)(2,1)S(1)}, u32[]{:S(2)}, u32[]{:S(2)}) collective-permute-start(bf16[16,2,8,512]{3,2,1,0:T(8,128)(2,1)S(1)} %all-to-all-done.same_ref), channel_id=1, source_target_pairs={{0,1},{1,0},{2,3},{3,2},{4,5},{5,4},{6,7},{7,6},{8,9},{9,8},{10,11... | collective-permute-start | bytes 786440 | tf_op jit(solution)/shard_map/ppermute | solution.py:228
